TPU v7x, 32 devices: a whole 2x2x4 slice. The times are simulated.
32 devices in a mesh: clips: 2 (over y), ctx: 8 (over z, x), head: 2 (over core).
Axes of the slice: x: 2, y: 2, z: 4, core: 2. Of those that a mesh axis runs over, the one named last changes fastest.
Arguments:
- query_in: bfloat16 [4096, 2560], P(('clips', 'ctx', 'head')), parts along dimension 0, may hold values from -6 to 6
- key_in: bfloat16 [4096, 2560], P(('clips', 'ctx', 'head')), parts along dimension 0, may hold values from -6 to 6
- value_in: bfloat16 [4096, 2560], P(('clips', 'ctx', 'head')), parts along dimension 0, may hold values from -6 to 6
- block_keep: int32 [2, 1, 8, 3, 3], P('clips'), parts along dimension 0, may hold values 0 or 1
Outputs:
- attended: bfloat16 [4096, 2560], P(('clips', 'ctx', 'head')), parts along dimension 0
There are 2 independent parts, one for each index of `clips`. A program takes and returns all parts, laid end to end along the dimension named above; each array names one. Nothing has to cross between parts.
All inputs are finite; a program needn't handle non-finite values.
Results may differ from a plain program's by a relative error of at most 0.0035.
Values may be sent and summed in bfloat16 or wider, within the bound.
A program may use at most 128 MiB of HBM per device.

v0:
```python
import jax
import jax.numpy as jnp
from jax import lax
from jax.sharding import PartitionSpec as P

HD = 128
TILE_S = 8
COLS = 64


NEG_BIG = -1e30


def swapped(block, axis, distance):
    count = lax.axis_size(axis)
    route = []
    for low in range(count):
        high = low | 1 << distance
        if high != low and high < count:
            route += [(low, high), (high, low)]
    return lax.ppermute(block, axis, route)


def from_behind(block, axis, distance):
    devices = range(lax.axis_size(axis))
    route = [(i - distance, i) for i in devices if i - distance in devices]
    return lax.ppermute(block, axis, route)


def order_pair(pair_side, mine, partner):
    first = jnp.where(pair_side == 0, mine, partner)
    second = jnp.where(pair_side == 0, partner, mine)
    return jnp.concatenate([first, second], axis=0)


def tile_flag(keep_pair, frame_at, col_at, frame_tiles, col_tiles, query_pos, frame_step, column):
    spot = column - query_pos + 1
    if frame_step == 1 and spot == 1:
        return jnp.array(True)
    frame_ok = (frame_at + frame_step - 1 >= 0) & (frame_at + frame_step - 1 < frame_tiles)
    col_ok = (col_at + column >= 0) & (col_at + column < col_tiles)
    return keep_pair[query_pos, frame_step, spot] & frame_ok & col_ok


def absorb(running, scores, allowed, mix_values):
    run_max, run_sum, run_out = running
    masked = jnp.where(allowed[None], scores, NEG_BIG)
    new_max = jnp.maximum(run_max, masked.max(-1))
    block_sum = jnp.where(allowed[None], jnp.exp(masked - new_max[..., None]), 0.0).sum(-1)
    weights_b = jnp.where(allowed[None], jnp.exp(masked - new_max[..., None]), 0.0).astype(
        jnp.bfloat16
    )
    factor = jnp.exp(run_max - new_max)
    new_sum = run_sum * factor + block_sum
    product = mix_values(weights_b)
    return (new_max, new_sum, run_out * factor[..., None] + product)


def inner_block(running, query_heads, key_pair, value_pair, tile_flags):
    tile_tok = key_pair.shape[0] // 2
    head_count = query_heads.shape[1]
    allowed = jnp.broadcast_to(tile_flags[:, None, :, None], (2, tile_tok, 2, tile_tok)).reshape(
        2 * tile_tok, 2 * tile_tok
    )
    key_rows = key_pair.reshape(2 * tile_tok, head_count, HD)
    value_rows = value_pair.reshape(2 * tile_tok, head_count, HD)
    scores = jnp.einsum(
        "qhd,khd->hqk", query_heads, key_rows, preferred_element_type=jnp.float32
    ) * HD ** (-0.5)

    def mix_values(weights_b):
        return jnp.einsum("hqk,khd->hqd", weights_b, value_rows, preferred_element_type=jnp.float32)

    return absorb(running, scores, allowed, mix_values)


def outer_block(running, query_heads, key_groups, value_groups, tile_flags):
    tile_tok = key_groups.shape[1]
    head_count = query_heads.shape[1]
    allowed = jnp.broadcast_to(tile_flags[:, None, None], (2, tile_tok, tile_tok)).reshape(
        2 * tile_tok, tile_tok
    )
    query_groups = query_heads.reshape(2, tile_tok, head_count, HD)
    key_rows = key_groups.reshape(2, tile_tok, head_count, HD)
    value_rows = value_groups.reshape(2, tile_tok, head_count, HD)
    scores = jnp.einsum(
        "gqhd,gkhd->hgqk", query_groups, key_rows, preferred_element_type=jnp.float32
    ) * HD ** (-0.5)
    scores = scores.reshape(head_count, 2 * tile_tok, tile_tok)

    def mix_values(weights_b):
        grouped = weights_b.reshape(head_count, 2, tile_tok, tile_tok)
        mixed = jnp.einsum(
            "hgqk,gkhd->hgqd", grouped, value_rows, preferred_element_type=jnp.float32
        )
        return mixed.reshape(head_count, 2 * tile_tok, HD)

    return absorb(running, scores, allowed, mix_values)


def local(query_in, key_in, value_in, block_keep):
    ctx_count = lax.axis_size("ctx")
    ctx_place = lax.axis_index("ctx")
    col_tiles = COLS // TILE_S
    row_tiles = max(1, ctx_count // (4 * col_tiles))
    frame_tiles = ctx_count // (row_tiles * col_tiles)
    frame_stride = row_tiles * col_tiles
    query_full, key_full, value_full = (
        lax.all_to_all(query_in, "head", split_axis=1, concat_axis=0, tiled=True),
        lax.all_to_all(key_in, "head", split_axis=1, concat_axis=0, tiled=True),
        lax.all_to_all(value_in, "head", split_axis=1, concat_axis=0, tiled=True),
    )
    tile_tok = query_full.shape[0]
    half_width = query_full.shape[1] // 2
    head_count = half_width // HD
    pair_side = ctx_place % 2

    def part_of(array, which):
        return lax.dynamic_slice_in_dim(array, which * half_width, half_width, 1)

    other_side = 1 - pair_side
    got_query, got_key, got_value = swapped(
        (
            part_of(query_full, other_side),
            part_of(key_full, other_side),
            part_of(value_full, other_side),
        ),
        "ctx",
        0,
    )
    query_pair = order_pair(pair_side, part_of(query_full, pair_side), got_query)
    key_pair = order_pair(pair_side, part_of(key_full, pair_side), got_key)
    value_pair = order_pair(pair_side, part_of(value_full, pair_side), got_value)
    query_heads = query_pair.reshape(2 * tile_tok, head_count, HD)
    first_tile = ctx_place - pair_side
    frame_at = first_tile // frame_stride
    col_at = first_tile % col_tiles
    keep_all = (block_keep > 0).reshape(-1, 3, 3)
    keep_pair = lax.dynamic_slice_in_dim(keep_all, first_tile, 2, 0)

    def inner_flags(frame_step):
        rows_list = []
        for query_pos in (0, 1):
            rows_list.append(
                jnp.stack(
                    [
                        tile_flag(
                            keep_pair,
                            frame_at,
                            col_at,
                            frame_tiles,
                            col_tiles,
                            query_pos,
                            frame_step,
                            column,
                        )
                        for column in (0, 1)
                    ]
                )
            )
        return jnp.stack(rows_list)

    def outer_flags(frame_step):
        left_flag = tile_flag(
            keep_pair, frame_at, col_at, frame_tiles, col_tiles, 0, frame_step, -1
        )
        right_flag = tile_flag(
            keep_pair, frame_at, col_at, frame_tiles, col_tiles, 1, frame_step, 2
        )
        return jnp.stack([left_flag, right_flag])

    side_tiles = []
    for distance, which_tile in ((2, 1), (-2, 0)):
        sent_tile = (
            key_pair[which_tile * tile_tok : (which_tile + 1) * tile_tok],
            value_pair[which_tile * tile_tok : (which_tile + 1) * tile_tok],
        )
        side_tiles.append(from_behind((sent_tile[0], sent_tile[1]), "ctx", distance))
    left_tile, right_tile = side_tiles
    running = (
        jnp.full((head_count, 2 * tile_tok), NEG_BIG, jnp.float32),
        jnp.zeros((head_count, 2 * tile_tok), jnp.float32),
        jnp.zeros((head_count, 2 * tile_tok, HD), jnp.float32),
    )
    running = inner_block(running, query_heads, key_pair, value_pair, inner_flags(1))
    running = outer_block(
        running,
        query_heads,
        jnp.stack([left_tile[0], right_tile[0]]),
        jnp.stack([left_tile[1], right_tile[1]]),
        outer_flags(1),
    )
    for frame_step, distance in ((0, frame_stride), (2, -frame_stride)):
        near_key, near_value = from_behind((key_pair, value_pair), "ctx", distance)
        corners = []
        for offset, which_tile in ((2, 1), (-2, 0)):
            sent_tile = (
                key_pair[which_tile * tile_tok : (which_tile + 1) * tile_tok],
                value_pair[which_tile * tile_tok : (which_tile + 1) * tile_tok],
            )
            corners.append(from_behind((sent_tile[0], sent_tile[1]), "ctx", distance + offset))
        running = inner_block(running, query_heads, near_key, near_value, inner_flags(frame_step))
        running = outer_block(
            running,
            query_heads,
            jnp.stack([corners[0][0], corners[1][0]]),
            jnp.stack([corners[0][1], corners[1][1]]),
            outer_flags(frame_step),
        )
    run_max, run_sum, run_out = running
    finished = (run_out / run_sum[..., None]).astype(jnp.bfloat16)
    finished = finished.transpose(1, 0, 2).reshape(2 * tile_tok, head_count * HD)
    first_out = finished[:tile_tok]
    second_out = finished[tile_tok:]
    mine_out = jnp.where(pair_side == 0, first_out, second_out)
    partner_out = jnp.where(pair_side == 0, second_out, first_out)
    returned = swapped(partner_out, "ctx", 0)
    whole_tile = jnp.where(
        pair_side == 0,
        jnp.concatenate([mine_out, returned], axis=1),
        jnp.concatenate([returned, mine_out], axis=1),
    )
    return lax.all_to_all(whole_tile, "head", split_axis=0, concat_axis=1, tiled=True)


def solution(mesh):
    return jax.shard_map(
        local,
        mesh=mesh,
        in_specs=(
            P(("clips", "ctx", "head"), None),
            P(("clips", "ctx", "head"), None),
            P(("clips", "ctx", "head"), None),
            P("clips", None, None, None, None),
        ),
        out_specs=P(("clips", "ctx", "head"), None),
        check_vma=False,
    )
```

profile of v0, /device:TPU:25, one launch (start us, length us, event | category | flops | bytes accessed | tf_op | source)
XLA Modules:
  0.0 190.4 jit_solution(12322368784870568336)
XLA Ops:
  0.0 2.2 %copy.103 = bf16[128,2560]{0,1:T(8,128)(2,1)} copy(bf16[128,2560]{1,0:T(8,128)(2,1)} %param.5) | data formatting | bytes 1310720 | tf_op args[1]
  2.2 4.2 %all-to-all-start.1 = ((bf16[128,2,1280]{0,2,1:T(8,128)(2,1)}), bf16[128,2,1280]{0,2,1:T(8,128)(2,1)S(1)}, u32[]{:S(2)}, u32[]{:S(2)}) async-start(bf16[128,2,1280]{0,2,1:T(8,128)(2,1)} %bitcast.10), calls=%async_computation.1 | async-start | bytes 1310720 | tf_op jit(solution)/shard_map/all_to_all | solution.py:110
  6.4 1.5 all-to-all-done.1
  10.3 4.5 %all_to_all.73 = bf16[128,2,1280]{0,2,1:T(8,128)(2,1)S(1)} all-to-all(bf16[128,2,1280]{0,2,1:T(8,128)(2,1)S(1)} %bitcast.131), channel_id=1, replica_groups=mesh['clips'=2,'ctx'=8,'head'=2] {'head'}, dimensions={1} | all-to-all | bytes 1310720 | tf_op jit(solution)/shard_map/all_to_all | solution.py:109
  16.2 4.5 %all_to_all.74 = bf16[128,2,1280]{0,2,1:T(8,128)(2,1)S(1)} all-to-all(bf16[128,2,1280]{0,2,1:T(8,128)(2,1)S(1)} %bitcast.132), channel_id=1, replica_groups=mesh['clips'=2,'ctx'=8,'head'=2] {'head'}, dimensions={1} | all-to-all | bytes 1310720 | tf_op jit(solution)/shard_map/all_to_all | solution.py:111
  40.0 2.0 %broadcast_select_fusion.2 = (bf16[256,640]{0,1:T(8,128)(2,1)}, bf16[256,640]{0,1:T(8,128)(2,1)}) fusion(bf16[256,640]{0,1:T(8,128)(2,1)} %collective-permute-done.1, pred[]{:T(512)S(6)} %eq.5, bf16[256,1280]{0,1:T(8,128)(2,1)S(1)} %copy_bitcast_fusion.1, s32[]{:T(128)S(6)} %select_n.148), kind=kLoop, calls=%fused_computation.95 | loop fusion | flops 327680 | bytes 1310725 | tf_op jit(solution)/shard_map/jit(_where)/select_n | solution.py:32
  45.3 2.0 %pad_maximum_fusion.1 = bf16[512,640]{0,1:T(8,128)(2,1)} fusion(bf16[256,640]{0,1:T(8,128)(2,1)} %get-tuple-element.23, bf16[256,640]{0,1:T(8,128)(2,1)} %get-tuple-element.24), kind=kLoop, calls=%fused_computation.69 | loop fusion | flops 1310720 | bytes 1310720 | tf_op jit(solution)/shard_map/concatenate | solution.py:33
  47.2 4.1 %collective-permute-start.4 = (bf16[256,640]{0,1:T(8,128)(2,1)}, bf16[256,640]{0,1:T(8,128)(2,1)}, u32[]{:S(2)}, u32[]{:S(2)}) collective-permute-start(bf16[256,640]{0,1:T(8,128)(2,1)} %get-tuple-element.24), channel_id=1, source_target_pairs={{4,0},{6,2},{8,4},{10,6},{12,8},{14,10},{5,1},{7,3},{9,5},{11,7},{... | collective-permute-start | bytes 983048 | tf_op jit(solution)/shard_map/ppermute | solution.py:27
  52.5 4.6 %fusion = (f32[5,512]{1,0:T(8,128)S(1)}, f32[5,512,512]{1,2,0:T(8,128)}) fusion(pred[512,512]{0,1:T(8,128)(4,1)S(1)} %copy.100, bf16[512,5,128]{0,2,1:T(8,128)(2,1)S(1)} %bitcast.128, bf16[512,5,128]{0,2,1:T(8,128)(2,1)} %bitcast.12), kind=kOutput, calls=%fused_computation.6 | convolution fusion | flops 339473920 | bytes 6825984 | tf_op jit(solution)/shard_map/qhd,khd->hqk/dot_general | solution.py:67
  57.1 3.7 %collective-permute-start.13 = (bf16[256,640]{0,1:T(8,128)(2,1)}, bf16[256,640]{0,1:T(8,128)(2,1)}, u32[]{:S(2)}, u32[]{:S(2)}) collective-permute-start(bf16[256,640]{0,1:T(8,128)(2,1)} %get-tuple-element.23), channel_id=1, source_target_pairs={{12,0},{14,2},{13,1},{15,3},{28,16},{30,18},{29,17},{31,19}} | collective-permute-start | bytes 983048 | tf_op jit(solution)/shard_map/ppermute | solution.py:27
  60.8 1.9 %broadcast_select_fusion = (bf16[256,640]{0,1:T(8,128)(2,1)}, bf16[256,640]{0,1:T(8,128)(2,1)}) fusion(bf16[256,640]{0,1:T(8,128)(2,1)} %collective-permute-done.2, pred[]{:T(512)S(6)} %eq.5, bf16[256,1280]{0,1:T(8,128)(2,1)S(1)} %copy_bitcast_fusion, s32[]{:T(128)S(6)} %select_n.148), kind=kLoop, calls=%fused_computation.93 | loop fusion | flops 327680 | bytes 1310725 | tf_op jit(solution)/shard_map/jit(_where)/select_n | solution.py:32
  62.7 1.4 collective-permute-start.14
  65.4 4.7 %collective-permute-start.6 = (bf16[256,640]{0,1:T(8,128)(2,1)}, bf16[256,640]{0,1:T(8,128)(2,1)}, u32[]{:S(2)}, u32[]{:S(2)}) collective-permute-start(bf16[256,640]{0,1:T(8,128)(2,1)} %get-tuple-element.22), channel_id=1, source_target_pairs={{4,0},{6,2},{8,4},{10,6},{12,8},{14,10},{5,1},{7,3},{9,5},{11,7},{... | collective-permute-start | bytes 983048 | tf_op jit(solution)/shard_map/ppermute | solution.py:27
  70.1 2.0 %pad_maximum_fusion.2 = bf16[512,640]{0,1:T(8,128)(2,1)} fusion(bf16[256,640]{0,1:T(8,128)(2,1)} %get-tuple-element.21, bf16[256,640]{0,1:T(8,128)(2,1)} %get-tuple-element.22), kind=kLoop, calls=%fused_computation.70 | loop fusion | flops 1310720 | bytes 1310720 | tf_op jit(solution)/shard_map/concatenate | solution.py:33
  72.2 1.9 %copy.112 = bf16[2,256,5,128]{3,1,0,2:T(8,128)(2,1)} copy(bf16[2,256,5,128]{1,0,3,2:T(2,128)(2,1)S(1)} %reshape_reshape.2) | data formatting | bytes 1310720 | tf_op jit(solution)/shard_map/reshape;reshape | solution.py:83
  76.0 1.5 collective-permute-start.7
  77.5 2.4 %fusion.17 = (f32[5,2,256]{2,1,0:T(2,128)}, f32[5,2,256,256]{2,3,1,0:T(8,128)S(1)}) fusion(pred[2]{0:T(512)(128)(4,1)} %pad_add_fusion.3, bf16[2,256,5,128]{3,1,0,2:T(8,128)(2,1)} %copy.112, bf16[1,256,5,128]{3,1,0,2:T(8,128)(2,1)} %copy.122, bf16[1,256,5,128]{3,1,0,2:T(8,128)(2,1)} %copy.121), kind=kOutput, calls=%fused_computation.26 | convolution fusion | flops 170063360 | bytes 3942402 | tf_op jit(solution)/shard_map/gqhd,gkhd->hgqk/dot_general | solution.py:86
  79.9 1.9 copy.110
  81.8 1.9 copy.111
  83.6 1.5 collective-permute-start.11
  86.5 7.3 %collective-permute-start.15 = (bf16[256,640]{0,1:T(8,128)(2,1)}, bf16[256,640]{0,1:T(8,128)(2,1)}, u32[]{:S(2)}, u32[]{:S(2)}) collective-permute-start(bf16[256,640]{0,1:T(8,128)(2,1)} %get-tuple-element.21), channel_id=1, source_target_pairs={{12,0},{14,2},{13,1},{15,3},{28,16},{30,18},{29,17},{31,19}} | collective-permute-start | bytes 983048 | tf_op jit(solution)/shard_map/ppermute | solution.py:27
  93.7 1.4 collective-permute-start.16
  95.1 3.3 %fusion.16 = (f32[5,2,256]{2,1,0:T(2,128)S(1)}, f32[5,2,256,256]{2,3,1,0:T(8,128)}) fusion(pred[2]{0:T(512)(128)(4,1)} %pad_add_fusion.1, bf16[2,256,5,128]{3,1,0,2:T(8,128)(2,1)} %copy.112, bf16[1,256,5,128]{3,1,0,2:T(8,128)(2,1)} %copy.111, bf16[1,256,5,128]{3,1,0,2:T(8,128)(2,1)} %copy.110), kind=kOutput, calls=%fused_computation.25 | convolution fusion | flops 170063360 | bytes 3942402 | tf_op jit(solution)/shard_map/gqhd,gkhd->hgqk/dot_general | solution.py:86
  99.7 1.9 copy.130
  101.5 1.9 copy.131
  103.4 3.4 %fusion.18 = (f32[5,2,256]{2,1,0:T(2,128)S(1)}, f32[5,2,256,256]{2,3,1,0:T(8,128)}) fusion(pred[2]{0:T(512)(128)(4,1)} %pad_add_fusion.5, bf16[2,256,5,128]{3,1,0,2:T(8,128)(2,1)} %copy.112, bf16[1,256,5,128]{3,1,0,2:T(8,128)(2,1)} %copy.131, bf16[1,256,5,128]{3,1,0,2:T(8,128)(2,1)} %copy.130), kind=kOutput, calls=%fused_computation.27 | convolution fusion | flops 170063360 | bytes 3942402 | tf_op jit(solution)/shard_map/gqhd,gkhd->hgqk/dot_general | solution.py:86
  108.0 1.9 copy.113
  109.9 1.9 copy.114
  111.7 1.5 collective-permute-start.8
  113.3 1.9 copy.124
  115.1 1.9 copy.125
  117.0 1.9 copy.133
  118.9 1.9 copy.134
  120.8 5.9 %select_reduce_fusion = (f32[5,512]{1,0:T(8,128)}, f32[5,512]{1,0:T(8,128)}, f32[5,512,512]{1,2,0:T(8,128)}) fusion(pred[512,512]{0,1:T(8,128)(4,1)} %copy.128, pred[512,512]{0,1:T(8,128)(4,1)} %copy.117, bf16[512,5,128]{0,2,1:T(8,128)(2,1)S(1)} %bitcast.129, bf16[512,5,128]{0,2,1:T(8,128)(2,1)} %bitcast.35), kind=kOutput, calls=%fused_computation.4 | convolution fusion | flops 342092800 | bytes 7098368 | tf_op jit(solution)/shard_map/qhd,khd->hqk/dot_general | solution.py:67
  128.1 1.4 fusion.133
  129.5 5.0 %fusion.3 = (f32[5,512]{1,0:T(8,128)}, f32[5,512]{1,0:T(8,128)}) fusion(f32[5,512,512]{1,2,0:T(8,128)} %get-tuple-element.49, f32[5,512]{1,0:T(8,128)S(1)} %get-tuple-element.17, pred[512,512]{0,1:T(8,128)(4,1)} %copy.117, f32[5,512]{1,0:T(8,128)S(1)} %get-tuple-element.15, pred[512,512]{0,1:T(8,128)(4,1)} %copy.128), kind=kLoop, calls=%fused_computation.9 | loop fusion | flops 11791360 | bytes 5808128 | tf_op jit(solution)/shard_map/reduce_sum | solution.py:49
  134.5 3.9 %fusion.9 = f32[5,512,128]{1,2,0:T(8,128)} fusion(bf16[512,5,128]{0,2,1:T(8,128)(2,1)} %bitcast.36, f32[5,512,512]{1,2,0:T(8,128)S(1)} %copy-done, f32[5,512]{1,0:T(8,128)S(1)} %get-tuple-element.17, pred[512,512]{0,1:T(8,128)(4,1)S(1)} %copy-done.6), kind=kOutput, calls=%fused_computation.20 | convolution fusion | flops 342097920 | bytes 7481344 | tf_op jit(solution)/shard_map/hqk,khd->hqd/dot_general | solution.py:72
  138.4 3.8 %fusion.7 = f32[5,512,128]{1,2,0:T(8,128)} fusion(bf16[512,5,128]{0,2,1:T(8,128)(2,1)} %bitcast.36, f32[5,512,512]{1,2,0:T(8,128)S(1)} %copy-done, f32[5,512]{1,0:T(8,128)S(1)} %get-tuple-element.15, pred[512,512]{0,1:T(8,128)(4,1)S(1)} %copy-done.7), kind=kOutput, calls=%fused_computation.19 | convolution fusion | flops 342097920 | bytes 7481344 | tf_op jit(solution)/shard_map/hqk,khd->hqd/dot_general | solution.py:72
  142.3 4.4 %fusion.1 = f32[5,512]{1,0:T(8,128)} fusion(f32[5,512,512]{1,2,0:T(8,128)} %get-tuple-element.55, f32[5,512]{1,0:T(8,128)S(1)} %get-tuple-element.30, pred[512,512]{0,1:T(8,128)(4,1)S(1)} %copy.100), kind=kLoop, calls=%fused_computation.7 | loop fusion | flops 6551040 | bytes 5525504 | tf_op jit(solution)/shard_map/reduce_sum | solution.py:49
  151.1 2.0 %fusion.62 = f32[5,2,256,128]{3,2,1,0:T(8,128)} fusion(f32[5,2,256,256]{2,3,1,0:T(8,128)S(1)} %copy-done.3, f32[5,2,256]{2,1,0:T(2,128)S(1)} %get-tuple-element.20, pred[2]{0:T(512)(128)(4,1)S(1)} %copy-done.32, bf16[1,256,5,128]{3,1,0,2:T(8,128)(2,1)S(1)} %copy-done.12, bf16[1,256,5,128]{3,1,0,2:T(8,128)(2,1)S(1)} %copy-done.11), kind=kOutput, calls=%fused_computation.47 | convolution fusion | flops 171376640 | bytes 4597762 | tf_op jit(solution)/shard_map/hgqk,gkhd->hgqd/dot_general | solution.py:93
  153.1 2.9 %copy.152 = f32[5,512,128]{1,2,0:T(8,128)} copy(f32[5,512,128]{2,1,0:T(8,128)} %bitcast.136) | data formatting | bytes 2621440 | tf_op jit(solution)/shard_map/reshape | solution.py:96
  156.1 2.7 %fusion.60 = f32[5,2,256,128]{3,2,1,0:T(8,128)} fusion(f32[5,2,256,256]{2,3,1,0:T(8,128)S(1)} %get-tuple-element.51, f32[5,2,256]{2,1,0:T(2,128)} %copy-done.28, pred[2]{0:T(512)(128)(4,1)} %pad_add_fusion.3, bf16[1,256,5,128]{3,1,0,2:T(8,128)(2,1)S(1)} %copy-done.14, bf16[1,256,5,128]{3,1,0,2:T(8,128)(2,1)S(1)} %copy-done.13), kind=kOutput, calls=%fused_computation.46 | convolution fusion | flops 171376640 | bytes 4597762 | tf_op jit(solution)/shard_map/hgqk,gkhd->hgqd/dot_general | solution.py:93
  158.7 3.0 %copy.153 = f32[5,512,128]{1,2,0:T(8,128)} copy(f32[5,512,128]{2,1,0:T(8,128)} %bitcast.137) | data formatting | bytes 2621440 | tf_op jit(solution)/shard_map/reshape | solution.py:96
  161.7 3.2 %fusion.58 = f32[5,2,256,128]{3,2,1,0:T(8,128)} fusion(f32[5,2,256,256]{2,3,1,0:T(8,128)S(1)} %copy-done.2, f32[5,2,256]{2,1,0:T(2,128)} %copy-done.27, pred[2]{0:T(512)(128)(4,1)} %pad_add_fusion.5, bf16[1,256,5,128]{3,1,0,2:T(8,128)(2,1)} %copy.134, bf16[1,256,5,128]{3,1,0,2:T(8,128)(2,1)} %copy.133), kind=kOutput, calls=%fused_computation.45 | convolution fusion | flops 171376640 | bytes 4597762 | tf_op jit(solution)/shard_map/hgqk,gkhd->hgqd/dot_general | solution.py:93
  164.9 2.9 %copy.154 = f32[5,512,128]{1,2,0:T(8,128)} copy(f32[5,512,128]{2,1,0:T(8,128)} %bitcast.138) | data formatting | bytes 2621440 | tf_op jit(solution)/shard_map/reshape | solution.py:96
  168.8 5.7 %fusion.81 = bf16[512,5,128]{0,2,1:T(8,128)(2,1)S(1)} fusion(f32[5,512,128]{1,2,0:T(8,128)} %copy.154, f32[5,512,128]{1,2,0:T(8,128)} %fusion.7, f32[5,512,128]{1,2,0:T(8,128)S(1)} %copy-done.5, f32[5,512,128]{1,2,0:T(8,128)} %fusion.9, f32[5,512,128]{1,2,0:T(8,128)S(1)} %copy-done.4, bf16[512,5,128]{0,2,1:T(8,128)(2,1)S(1)} %bitcast.143, ...), kind=kOutput, calls=%fused_computation.64 | convolution fusion | flops 346357760 | bytes 13451264 | tf_op jit(solution)/shard_map/hqk,khd->hqd/dot_general | solution.py:72
  176.0 5.6 %collective-permute-done.17 = bf16[256,640]{1,0:T(8,128)(2,1)S(1)} collective-permute-done((bf16[256,640]{1,0:T(8,128)(2,1)S(1)}, bf16[256,640]{1,0:T(8,128)(2,1)S(1)}, u32[]{:S(2)}, u32[]{:S(2)}) %collective-permute-start.17) | collective-permute-done | bytes 327712 | tf_op jit(solution)/shard_map/ppermute | solution.py:21
  182.1 7.1 %all_to_all.75 = bf16[2,128,1280]{1,2,0:T(8,128)(2,1)S(1)} all-to-all(bf16[2,128,1280]{1,2,0:T(8,128)(2,1)S(1)} %copy.140), channel_id=1, replica_groups=mesh['clips'=2,'ctx'=8,'head'=2] {'head'}, dimensions={0} | all-to-all | bytes 1310720 | tf_op jit(solution)/shard_map/all_to_all | solution.py:223
  (147 shorter events, 34.1 us)
Async XLA Ops:
  0.0 9.9 %copy-start.8 = (bf16[128,2560]{1,0:T(8,128)(2,1)S(1)}, bf16[128,2560]{1,0:T(8,128)(2,1)}, u32[]{:S(2)}) copy-start(bf16[128,2560]{1,0:T(8,128)(2,1)} %param.4) | copy-start | bytes 1966084
  2.2 5.6 %all-to-all-start.1 = ((bf16[128,2,1280]{0,2,1:T(8,128)(2,1)}), bf16[128,2,1280]{0,2,1:T(8,128)(2,1)S(1)}, u32[]{:S(2)}, u32[]{:S(2)}) async-start(bf16[128,2,1280]{0,2,1:T(8,128)(2,1)} %bitcast.10), calls=%async_computation.1 | async-start | bytes 1310720 | tf_op jit(solution)/shard_map/all_to_all | solution.py:110
  8.0 8.0 %copy-start.9 = (bf16[128,2560]{1,0:T(8,128)(2,1)S(1)}, bf16[128,2560]{1,0:T(8,128)(2,1)}, u32[]{:S(2)}) copy-start(bf16[128,2560]{1,0:T(8,128)(2,1)} %param.6) | copy-start | bytes 1966084
  8.7 31.3 %collective-permute-start.1 = (bf16[256,640]{0,1:T(8,128)(2,1)}, bf16[256,640]{0,1:T(8,128)(2,1)}, u32[]{:S(2)}, u32[]{:S(2)}) collective-permute-start(bf16[256,640]{0,1:T(8,128)(2,1)} %constant_dynamic-slice_fusion.1), channel_id=1, source_target_pairs={{0,2},{2,0},{4,6},{6,4},{8,10},{10,8},{12,14},{14,12},{1,3},{3,1},... | collective-permute-start | bytes 983048 | tf_op jit(solution)/shard_map/ppermute | solution.py:21
  14.9 8.0 %copy-start.29 = (s32[1,1,8,3,3]{2,1,4,3,0:T(1,128)S(1)}, s32[1,1,8,3,3]{2,1,4,3,0:T(1,128)}, u32[]{:S(2)}) copy-start(s32[1,1,8,3,3]{2,1,4,3,0:T(1,128)} %param.7) | copy-start | bytes 868
  15.7 31.6 %collective-permute-start = (bf16[256,640]{0,1:T(8,128)(2,1)}, bf16[256,640]{0,1:T(8,128)(2,1)}, u32[]{:S(2)}, u32[]{:S(2)}) collective-permute-start(bf16[256,640]{0,1:T(8,128)(2,1)} %constant_dynamic-slice_fusion.2), channel_id=1, source_target_pairs={{0,2},{2,0},{4,6},{6,4},{8,10},{10,8},{12,14},{14,12},{1,3},{3,1},... | collective-permute-start | bytes 983048 | tf_op jit(solution)/shard_map/ppermute | solution.py:21
  21.6 35.4 %collective-permute-start.2 = (bf16[256,640]{0,1:T(8,128)(2,1)}, bf16[256,640]{0,1:T(8,128)(2,1)}, u32[]{:S(2)}, u32[]{:S(2)}) collective-permute-start(bf16[256,640]{0,1:T(8,128)(2,1)} %constant_dynamic-slice_fusion), channel_id=1, source_target_pairs={{0,2},{2,0},{4,6},{6,4},{8,10},{10,8},{12,14},{14,12},{1,3},{3,1},... | collective-permute-start | bytes 983048 | tf_op jit(solution)/shard_map/ppermute | solution.py:21
  42.0 20.7 %collective-permute-start.9 = (bf16[256,640]{0,1:T(8,128)(2,1)}, bf16[256,640]{0,1:T(8,128)(2,1)S(1)}, u32[]{:S(2)}, u32[]{:S(2)}) collective-permute-start(bf16[256,640]{0,1:T(8,128)(2,1)} %get-tuple-element.23), channel_id=1, source_target_pairs={} | collective-permute-start | bytes 983048 | tf_op jit(solution)/shard_map/ppermute | solution.py:27
  42.7 22.7 %collective-permute-start.3 = (bf16[256,640]{0,1:T(8,128)(2,1)}, bf16[256,640]{0,1:T(8,128)(2,1)S(1)}, u32[]{:S(2)}, u32[]{:S(2)}) collective-permute-start(bf16[256,640]{0,1:T(8,128)(2,1)} %get-tuple-element.23), channel_id=1, source_target_pairs={{0,4},{2,6},{4,8},{6,10},{8,12},{10,14},{1,5},{3,7},{5,9},{7,11},{... | collective-permute-start | bytes 983048 | tf_op jit(solution)/shard_map/ppermute | solution.py:27
  44.0 20.1 %collective-permute-start.10 = (bf16[256,640]{0,1:T(8,128)(2,1)}, bf16[256,640]{0,1:T(8,128)(2,1)S(1)}, u32[]{:S(2)}, u32[]{:S(2)}) collective-permute-start(bf16[256,640]{0,1:T(8,128)(2,1)} %get-tuple-element.24), channel_id=1, source_target_pairs={{0,12},{2,14},{1,13},{3,15},{16,28},{18,30},{17,29},{19,31}} | collective-permute-start | bytes 983048 | tf_op jit(solution)/shard_map/ppermute | solution.py:27
  47.2 28.7 %collective-permute-start.4 = (bf16[256,640]{0,1:T(8,128)(2,1)}, bf16[256,640]{0,1:T(8,128)(2,1)}, u32[]{:S(2)}, u32[]{:S(2)}) collective-permute-start(bf16[256,640]{0,1:T(8,128)(2,1)} %get-tuple-element.24), channel_id=1, source_target_pairs={{4,0},{6,2},{8,4},{10,6},{12,8},{14,10},{5,1},{7,3},{9,5},{11,7},{... | collective-permute-start | bytes 983048 | tf_op jit(solution)/shard_map/ppermute | solution.py:27
  57.1 26.6 %collective-permute-start.13 = (bf16[256,640]{0,1:T(8,128)(2,1)}, bf16[256,640]{0,1:T(8,128)(2,1)}, u32[]{:S(2)}, u32[]{:S(2)}) collective-permute-start(bf16[256,640]{0,1:T(8,128)(2,1)} %get-tuple-element.23), channel_id=1, source_target_pairs={{12,0},{14,2},{13,1},{15,3},{28,16},{30,18},{29,17},{31,19}} | collective-permute-start | bytes 983048 | tf_op jit(solution)/shard_map/ppermute | solution.py:27
  62.7 22.4 %collective-permute-start.14 = (bf16[256,640]{0,1:T(8,128)(2,1)}, bf16[256,640]{0,1:T(8,128)(2,1)}, u32[]{:S(2)}, u32[]{:S(2)}) collective-permute-start(bf16[256,640]{0,1:T(8,128)(2,1)} %get-tuple-element.24), channel_id=1, source_target_pairs={} | collective-permute-start | bytes 983048 | tf_op jit(solution)/shard_map/ppermute | solution.py:27
  64.1 6.0 %copy-start.16 = (bf16[256,640]{0,1:T(8,128)(2,1)}, bf16[256,640]{0,1:T(8,128)(2,1)S(1)}, u32[]{:S(2)}) copy-start(bf16[256,640]{0,1:T(8,128)(2,1)S(1)} %collective-permute-done.10) | copy-start | bytes 983044
  64.1 22.4 %collective-permute-start.5 = (bf16[256,640]{0,1:T(8,128)(2,1)}, bf16[256,640]{0,1:T(8,128)(2,1)}, u32[]{:S(2)}, u32[]{:S(2)}) collective-permute-start(bf16[256,640]{0,1:T(8,128)(2,1)} %get-tuple-element.21), channel_id=1, source_target_pairs={{0,4},{2,6},{4,8},{6,10},{8,12},{10,14},{1,5},{3,7},{5,9},{7,11},{... | collective-permute-start | bytes 983048 | tf_op jit(solution)/shard_map/ppermute | solution.py:27
  65.4 10.6 %copy-start.15 = (bf16[256,640]{0,1:T(8,128)(2,1)}, bf16[256,640]{0,1:T(8,128)(2,1)S(1)}, u32[]{:S(2)}) copy-start(bf16[256,640]{0,1:T(8,128)(2,1)S(1)} %collective-permute-done.3) | copy-start | bytes 983044
  65.4 28.3 %collective-permute-start.6 = (bf16[256,640]{0,1:T(8,128)(2,1)}, bf16[256,640]{0,1:T(8,128)(2,1)}, u32[]{:S(2)}, u32[]{:S(2)}) collective-permute-start(bf16[256,640]{0,1:T(8,128)(2,1)} %get-tuple-element.22), channel_id=1, source_target_pairs={{4,0},{6,2},{8,4},{10,6},{12,8},{14,10},{5,1},{7,3},{9,5},{11,7},{... | collective-permute-start | bytes 983048 | tf_op jit(solution)/shard_map/ppermute | solution.py:27
  72.1 3.0 %copy-start.17 = (bf16[256,640]{0,1:T(8,128)(2,1)S(1)}, bf16[256,640]{0,1:T(8,128)(2,1)}, u32[]{:S(2)}) copy-start(bf16[256,640]{0,1:T(8,128)(2,1)} %copy-done.16) | copy-start | bytes 983044
  76.0 44.8 %collective-permute-start.7 = (bf16[512,640]{0,1:T(8,128)(2,1)}, bf16[512,640]{0,1:T(8,128)(2,1)}, u32[]{:S(2)}, u32[]{:S(2)}) collective-permute-start(bf16[512,640]{0,1:T(8,128)(2,1)} %pad_maximum_fusion.1), channel_id=1, source_target_pairs={} | collective-permute-start | bytes 1966088 | tf_op jit(solution)/shard_map/ppermute | solution.py:27
  83.6 14.8 %copy-start.21 = (f32[5,2,256]{2,1,0:T(2,128)S(1)}, f32[5,2,256]{2,1,0:T(2,128)}, u32[]{:S(2)}) copy-start(f32[5,2,256]{2,1,0:T(2,128)} %get-tuple-element.50) | copy-start | bytes 30724
  83.6 28.1 %collective-permute-start.11 = (bf16[256,640]{0,1:T(8,128)(2,1)}, bf16[256,640]{0,1:T(8,128)(2,1)}, u32[]{:S(2)}, u32[]{:S(2)}) collective-permute-start(bf16[256,640]{0,1:T(8,128)(2,1)} %get-tuple-element.21), channel_id=1, source_target_pairs={} | collective-permute-start | bytes 983048 | tf_op jit(solution)/shard_map/ppermute | solution.py:27
  85.2 30.0 %collective-permute-start.12 = (bf16[256,640]{0,1:T(8,128)(2,1)}, bf16[256,640]{0,1:T(8,128)(2,1)}, u32[]{:S(2)}, u32[]{:S(2)}) collective-permute-start(bf16[256,640]{0,1:T(8,128)(2,1)} %get-tuple-element.22), channel_id=1, source_target_pairs={{0,12},{2,14},{1,13},{3,15},{16,28},{18,30},{17,29},{19,31}} | collective-permute-start | bytes 983048 | tf_op jit(solution)/shard_map/ppermute | solution.py:27
  86.5 30.5 %collective-permute-start.15 = (bf16[256,640]{0,1:T(8,128)(2,1)}, bf16[256,640]{0,1:T(8,128)(2,1)}, u32[]{:S(2)}, u32[]{:S(2)}) collective-permute-start(bf16[256,640]{0,1:T(8,128)(2,1)} %get-tuple-element.21), channel_id=1, source_target_pairs={{12,0},{14,2},{13,1},{15,3},{28,16},{30,18},{29,17},{31,19}} | collective-permute-start | bytes 983048 | tf_op jit(solution)/shard_map/ppermute | solution.py:27
  93.7 25.2 %collective-permute-start.16 = (bf16[256,640]{0,1:T(8,128)(2,1)}, bf16[256,640]{0,1:T(8,128)(2,1)}, u32[]{:S(2)}, u32[]{:S(2)}) collective-permute-start(bf16[256,640]{0,1:T(8,128)(2,1)} %get-tuple-element.22), channel_id=1, source_target_pairs={} | collective-permute-start | bytes 983048 | tf_op jit(solution)/shard_map/ppermute | solution.py:27
  111.7 22.8 %collective-permute-start.8 = (bf16[512,640]{0,1:T(8,128)(2,1)}, bf16[512,640]{0,1:T(8,128)(2,1)}, u32[]{:S(2)}, u32[]{:S(2)}) collective-permute-start(bf16[512,640]{0,1:T(8,128)(2,1)} %pad_maximum_fusion.2), channel_id=1, source_target_pairs={} | collective-permute-start | bytes 1966088 | tf_op jit(solution)/shard_map/ppermute | solution.py:27
  129.5 5.0 %copy-start.19 = (f32[5,512]{1,0:T(8,128)}, f32[5,512]{1,0:T(8,128)S(1)}, u32[]{:S(2)}) copy-start(f32[5,512]{1,0:T(8,128)S(1)} %get-tuple-element.17) | copy-start | bytes 30724
  129.5 8.9 %copy-start.18 = (f32[5,512]{1,0:T(8,128)}, f32[5,512]{1,0:T(8,128)S(1)}, u32[]{:S(2)}) copy-start(f32[5,512]{1,0:T(8,128)S(1)} %get-tuple-element.15) | copy-start | bytes 30724
  129.5 12.7 %copy-start.20 = (f32[5,512]{1,0:T(8,128)}, f32[5,512]{1,0:T(8,128)S(1)}, u32[]{:S(2)}) copy-start(f32[5,512]{1,0:T(8,128)S(1)} %get-tuple-element.30) | copy-start | bytes 30724
  129.5 5.0 %copy-start = (f32[5,512,512]{1,2,0:T(8,128)S(1)}, f32[5,512,512]{1,2,0:T(8,128)}, u32[]{:S(2)}) copy-start(f32[5,512,512]{1,2,0:T(8,128)} %get-tuple-element.49) | copy-start | bytes 15728644
  129.5 5.0 %copy-start.6 = (pred[512,512]{0,1:T(8,128)(4,1)S(1)}, pred[512,512]{0,1:T(8,128)(4,1)}, u32[]{:S(2)}) copy-start(pred[512,512]{0,1:T(8,128)(4,1)} %copy.117) | copy-start | bytes 786436
  134.5 3.9 %copy-start.7 = (pred[512,512]{0,1:T(8,128)(4,1)S(1)}, pred[512,512]{0,1:T(8,128)(4,1)}, u32[]{:S(2)}) copy-start(pred[512,512]{0,1:T(8,128)(4,1)} %copy.128) | copy-start | bytes 786436
  142.3 4.4 %copy-start.22 = (f32[5,2,256]{2,1,0:T(2,128)S(1)}, f32[5,2,256]{2,1,0:T(2,128)}, u32[]{:S(2)}) copy-start(f32[5,2,256]{2,1,0:T(2,128)} %get-tuple-element.50) | copy-start | bytes 30724
  142.3 4.4 %copy-start.24 = (f32[5,2,256]{2,1,0:T(2,128)S(1)}, f32[5,2,256]{2,1,0:T(2,128)}, u32[]{:S(2)}) copy-start(f32[5,2,256]{2,1,0:T(2,128)} %copy-done.23) | copy-start | bytes 30724
  142.3 4.4 %copy-start.26 = (f32[5,2,256]{2,1,0:T(2,128)S(1)}, f32[5,2,256]{2,1,0:T(2,128)}, u32[]{:S(2)}) copy-start(f32[5,2,256]{2,1,0:T(2,128)} %copy-done.25) | copy-start | bytes 30724
  142.3 4.4 %copy-start.31 = (pred[2]{0:T(512)(128)(4,1)S(1)}, pred[2]{0:T(512)(128)(4,1)}, u32[]{:S(2)}) copy-start(pred[2]{0:T(512)(128)(4,1)} %pad_add_fusion.3) | copy-start | bytes 10
  146.7 2.4 %copy-start.28 = (f32[5,2,256]{2,1,0:T(2,128)}, f32[5,2,256]{2,1,0:T(2,128)S(1)}, u32[]{:S(2)}) copy-start(f32[5,2,256]{2,1,0:T(2,128)S(1)} %get-tuple-element.19) | copy-start | bytes 30724
  146.7 3.0 %copy-start.27 = (f32[5,2,256]{2,1,0:T(2,128)}, f32[5,2,256]{2,1,0:T(2,128)S(1)}, u32[]{:S(2)}) copy-start(f32[5,2,256]{2,1,0:T(2,128)S(1)} %get-tuple-element.18) | copy-start | bytes 30724
  146.8 3.0 %copy-start.1 = (f32[5,2,256,256]{2,3,1,0:T(8,128)S(1)}, f32[5,2,256,256]{2,3,1,0:T(8,128)}, u32[]{:S(2)}) copy-start(f32[5,2,256,256]{2,3,1,0:T(8,128)} %get-tuple-element.48) | copy-start | bytes 7864324
  146.8 3.0 %copy-start.30 = (pred[2]{0:T(512)(128)(4,1)S(1)}, pred[2]{0:T(512)(128)(4,1)}, u32[]{:S(2)}) copy-start(pred[2]{0:T(512)(128)(4,1)} %pad_add_fusion.5) | copy-start | bytes 10
  148.4 2.7 %copy-start.11 = (bf16[1,256,5,128]{3,1,0,2:T(8,128)(2,1)S(1)}, bf16[1,256,5,128]{3,1,0,2:T(8,128)(2,1)}, u32[]{:S(2)}) copy-start(bf16[1,256,5,128]{3,1,0,2:T(8,128)(2,1)} %copy.113) | copy-start | bytes 983044
  148.4 2.7 %copy-start.12 = (bf16[1,256,5,128]{3,1,0,2:T(8,128)(2,1)S(1)}, bf16[1,256,5,128]{3,1,0,2:T(8,128)(2,1)}, u32[]{:S(2)}) copy-start(bf16[1,256,5,128]{3,1,0,2:T(8,128)(2,1)} %copy.114) | copy-start | bytes 983044
  153.1 2.9 %copy-start.13 = (bf16[1,256,5,128]{3,1,0,2:T(8,128)(2,1)S(1)}, bf16[1,256,5,128]{3,1,0,2:T(8,128)(2,1)}, u32[]{:S(2)}) copy-start(bf16[1,256,5,128]{3,1,0,2:T(8,128)(2,1)} %copy.124) | copy-start | bytes 983044
  153.1 2.9 %copy-start.14 = (bf16[1,256,5,128]{3,1,0,2:T(8,128)(2,1)S(1)}, bf16[1,256,5,128]{3,1,0,2:T(8,128)(2,1)}, u32[]{:S(2)}) copy-start(bf16[1,256,5,128]{3,1,0,2:T(8,128)(2,1)} %copy.125) | copy-start | bytes 983044
  158.7 3.0 %copy-start.2 = (f32[5,2,256,256]{2,3,1,0:T(8,128)S(1)}, f32[5,2,256,256]{2,3,1,0:T(8,128)}, u32[]{:S(2)}) copy-start(f32[5,2,256,256]{2,3,1,0:T(8,128)} %get-tuple-element.48) | copy-start | bytes 7864324
  161.7 7.1 %copy-start.10 = (bf16[512,640]{0,1:T(8,128)(2,1)S(1)}, bf16[512,640]{0,1:T(8,128)(2,1)}, u32[]{:S(2)}) copy-start(bf16[512,640]{0,1:T(8,128)(2,1)} %pad_maximum_fusion.2) | copy-start | bytes 1966084
  164.9 3.8 %copy-start.4 = (f32[5,512,128]{1,2,0:T(8,128)S(1)}, f32[5,512,128]{1,2,0:T(8,128)}, u32[]{:S(2)}) copy-start(f32[5,512,128]{1,2,0:T(8,128)} %copy.152) | copy-start | bytes 3932164
  164.9 3.8 %copy-start.5 = (f32[5,512,128]{1,2,0:T(8,128)S(1)}, f32[5,512,128]{1,2,0:T(8,128)}, u32[]{:S(2)}) copy-start(f32[5,512,128]{1,2,0:T(8,128)} %copy.153) | copy-start | bytes 3932164
  174.7 6.9 %collective-permute-start.17 = (bf16[256,640]{1,0:T(8,128)(2,1)S(1)}, bf16[256,640]{1,0:T(8,128)(2,1)S(1)}, u32[]{:S(2)}, u32[]{:S(2)}) collective-permute-start(bf16[256,640]{1,0:T(8,128)(2,1)S(1)} %copy.137), channel_id=1, source_target_pairs={{0,2},{2,0},{4,6},{6,4},{8,10},{10,8},{12,14},{14,12},{1,3},{3,1},... | collective-permute-start | bytes 983048 | tf_op jit(solution)/shard_map/ppermute | solution.py:21
  (4 other events, 4.7 us)
where the time goes:
time: 192 us; the launch traced here: 190 us
  local copies, waits for them, and re-layouts  50.3 us (26%)
  matrix products  40.8 us (21%)
  starting transfers between devices  40.1 us (21%)
  other arithmetic  25.2 us (13%)
  blocking collectives  16.2 us (8%)
  between operations  10.6 us (6%)
  waiting for transfers between devices  7.13 us (4%)
    ppermute x14, starting transfers between devices, from_behind(): return lax.ppermute(block, axis, route)  32.9 us
    dot_general x3, matrix products, mix_values(): jnp.einsum('hqk,khd->hqd', weights_b, value_rows, preferred_element_type=...  13.4 us
    reduce_sum x5, other arithmetic, absorb(): jnp.where(allowed[None], jnp.exp(masked - new_max[..., None]), 0.0).sum(-1)  11.5 us
    dot_general x2, matrix products, inner_block(): jnp.einsum('qhd,khd->hqk', query_heads, key_rows, preferred_element_type=...  10.4 us
    dot_general x3, matrix products, outer_block(): jnp.einsum('gqhd,gkhd->hgqk', query_groups, key_rows, preferred_element_t...  9.1 us
    reshape x3, local copies, waits for them, and re-layouts, mix_values(): return mixed.reshape(head_count, 2 * tile_tok, HD)  8.79 us
    unnamed x78, local copies, waits for them, and re-layouts  7.96 us
    dot_general x3, matrix products, mix_values(): jnp.einsum('hgqk,gkhd->hgqd', grouped, value_rows, preferred_element_type...  7.93 us
  transfers between devices with their start and end apart: 19, of which 2 were waited for; matrix products, arithmetic and copies ran while one was open for 37% of the time, Pallas kernels for 0%

commit v1 on v0

--- a/solution.py
+++ b/solution.py
@@ -1,6 +1,10 @@
+import functools
+
 import jax
 import jax.numpy as jnp
 from jax import lax
+from jax.experimental import pallas as pl
+from jax.experimental.pallas import tpu as pltpu
 from jax.sharding import PartitionSpec as P
 
 HD = 128
@@ -223,9 +227,238 @@
     return lax.all_to_all(whole_tile, "head", split_axis=0, concat_axis=1, tiled=True)
 
 
+HEADS_A_CHUNK = 2
+LOG2_E = 1.4426950408889634
+MESH = pl.DeviceIdType.MESH
+OWN, CORE, BESIDE, BESIDE_CORE, FAR, FAR_CORE = range(6)
+
+
+def attend(query, keys, values, beside_ok, far_ok, tile_tok):
+    scale = HD ** (-0.5) * LOG2_E
+    scores = lax.dot_general(
+        query, keys, (((1,), (1,)), ((), ())), preferred_element_type=jnp.float32
+    )
+    own, beside, far = (scores[:, i * tile_tok : (i + 1) * tile_tok] for i in range(3))
+    row_max = jnp.maximum(
+        own.max(-1, keepdims=True),
+        jnp.maximum(
+            jnp.where(beside_ok, beside.max(-1, keepdims=True), NEG_BIG),
+            jnp.where(far_ok, far.max(-1, keepdims=True), NEG_BIG),
+        ),
+    )
+    weights = jnp.concatenate(
+        [
+            jnp.exp2((own - row_max) * scale),
+            jnp.exp2((beside - jnp.where(beside_ok, row_max, -NEG_BIG)) * scale),
+            jnp.exp2((far - jnp.where(far_ok, row_max, -NEG_BIG)) * scale),
+        ],
+        axis=1,
+    )
+    row_sum = weights.sum(-1, keepdims=True)
+    mixed = jnp.dot(weights.astype(jnp.bfloat16), values, preferred_element_type=jnp.float32)
+    return (mixed / row_sum).astype(jnp.bfloat16)
+
+
+def row_kernel(
+    tiles, heads_a_chunk,
+    query_in, key_in, value_in, keep, out,
+    query, pairs, result, load_sem, store_sem, send_sem, recv_sem,
+):
+    rows = query_in.shape[0]
+    chunks = query_in.shape[1] // (heads_a_chunk * HD)
+    width = heads_a_chunk * HD
+    clip, tile, core = lax.axis_index("clips"), lax.axis_index("ctx"), lax.axis_index("head")
+    side = lax.rem(tile, 2)
+    step = 2 - 4 * side
+    to_far, from_far = tile + step, tile - step
+    sends_far = jnp.logical_and(to_far >= 0, to_far < tiles)
+    gets_far = jnp.logical_and(from_far >= 0, from_far < tiles)
+    other_core = (clip, tile, 1 - core)
+    paired = (clip, tile + 1 - 2 * side, core)
+    beyond = (clip, jnp.where(sends_far, to_far, tile), core)
+    behind = (clip, jnp.where(gets_far, from_far, tile), core)
+
+    def place(slot):
+        return pl.ds(slot * rows, rows)
+
+    def columns(chunk):
+        return pl.ds(pl.multiple_of(chunk * width, width), width)
+
+    def own_copy(which, kind, slot, device, chunk):
+        source = (key_in, value_in)[which]
+        return pltpu.make_async_remote_copy(
+            src_ref=source.at[:, columns(chunk)],
+            dst_ref=pairs.at[which, place(slot), columns(chunk)],
+            send_sem=send_sem.at[kind + which, chunk],
+            recv_sem=recv_sem.at[kind + which, chunk],
+            device_id=device,
+            device_id_type=MESH,
+        )
+
+    def relay(kind, source, slot, device, chunk):
+        return pltpu.make_async_remote_copy(
+            src_ref=pairs.at[:, place(source), columns(chunk)],
+            dst_ref=pairs.at[:, place(slot), columns(chunk)],
+            send_sem=send_sem.at[kind, chunk],
+            recv_sem=recv_sem.at[kind, chunk],
+            device_id=device,
+            device_id_type=MESH,
+        )
+
+    def to_core(which, chunk):
+        return own_copy(which, 0, CORE, other_core, chunk)
+
+    def to_paired(which, chunk):
+        return own_copy(which, 2, BESIDE, paired, chunk)
+
+    def paired_to_core(chunk):
+        return relay(4, BESIDE, BESIDE_CORE, other_core, chunk)
+
+    def paired_to_far(chunk):
+        return relay(5, BESIDE, FAR, beyond, chunk)
+
+    def far_to_core(chunk):
+        return relay(6, FAR, FAR_CORE, other_core, chunk)
+
+    def store(chunk):
+        return pltpu.make_async_copy(
+            result.at[:, columns(chunk)], out.at[:, columns(chunk)], store_sem.at[chunk]
+        )
+
+    loads = (
+        pltpu.make_async_copy(query_in, query, load_sem.at[0]),
+        pltpu.make_async_copy(key_in, pairs.at[0, place(OWN)], load_sem.at[1]),
+        pltpu.make_async_copy(value_in, pairs.at[1, place(OWN)], load_sem.at[2]),
+    )
+
+    barrier = pltpu.get_barrier_semaphore()
+    pl.semaphore_signal(barrier, inc=1, device_id=other_core, device_id_type=MESH)
+    pl.semaphore_signal(barrier, inc=1, device_id=paired, device_id_type=MESH)
+
+    @pl.when(sends_far)
+    def _():
+        pl.semaphore_signal(barrier, inc=1, device_id=beyond, device_id_type=MESH)
+
+    @pl.when(gets_far)
+    def _():
+        pl.semaphore_signal(barrier, inc=1, device_id=behind, device_id_type=MESH)
+
+    for load in loads:
+        load.start()
+
+    @pl.when(jnp.logical_not(gets_far))
+    def _():
+        pairs[:, pl.ds(FAR * rows, 2 * rows), :] = jnp.zeros(
+            (2, 2 * rows, pairs.shape[2]), pairs.dtype
+        )
+
+    pl.semaphore_wait(
+        barrier, 2 + sends_far.astype(jnp.int32) + gets_far.astype(jnp.int32)
+    )
+
+    @pl.loop(0, chunks)
+    def _(chunk):
+        for which in range(2):
+            to_paired(which, chunk).start()
+        for which in range(2):
+            to_core(which, chunk).start()
+
+    for load in loads:
+        load.wait()
+
+    beside_ok = jnp.where(side == 0, keep[0, 0, tile, 1, 2], keep[0, 0, tile, 1, 0]) > 0
+    far_ok = jnp.logical_and(
+        jnp.where(side == 0, keep[0, 0, tile, 1, 0], keep[0, 0, tile, 1, 2]) > 0, gets_far
+    )
+
+    @pl.loop(0, chunks + 2)
+    def _(turn):
+        @pl.when(turn < chunks)
+        def _():
+            for which in range(2):
+                to_paired(which, turn).wait_recv()
+            paired_to_core(turn).start()
+
+            @pl.when(sends_far)
+            def _():
+                paired_to_far(turn).start()
+
+        @pl.when(jnp.logical_and(jnp.logical_and(turn >= 1, turn <= chunks), gets_far))
+        def _():
+            paired_to_far(turn - 1).wait_recv()
+            far_to_core(turn - 1).start()
+
+        @pl.when(turn >= 2)
+        def _():
+            chunk = turn - 2
+            for which in range(2):
+                to_core(which, chunk).wait_recv()
+            paired_to_core(chunk).wait_recv()
+
+            @pl.when(gets_far)
+            def _():
+                far_to_core(chunk).wait_recv()
+
+            for head in range(heads_a_chunk):
+                at = pl.ds(pl.multiple_of(chunk * width + head * HD, HD), HD)
+                result[:, at] = attend(
+                    query[:, at], pairs[0, :, at], pairs[1, :, at], beside_ok, far_ok, 2 * rows
+                )
+            store(chunk).start()
+
+    @pl.loop(0, chunks)
+    def _(chunk):
+        for which in range(2):
+            to_core(which, chunk).wait_send()
+            to_paired(which, chunk).wait_send()
+        paired_to_core(chunk).wait_send()
+
+        @pl.when(sends_far)
+        def _():
+            paired_to_far(chunk).wait_send()
+
+        @pl.when(gets_far)
+        def _():
+            far_to_core(chunk).wait_send()
+
+        store(chunk).wait()
+
+
+def one_row(query_in, key_in, value_in, block_keep):
+    rows, width = query_in.shape
+    heads = width // HD
+    heads_a_chunk = HEADS_A_CHUNK
+    chunks = heads // heads_a_chunk
+    return pl.pallas_call(
+        functools.partial(row_kernel, lax.axis_size("ctx"), heads_a_chunk),
+        out_shape=jax.ShapeDtypeStruct((rows, width), jnp.bfloat16),
+        in_specs=[pl.BlockSpec(memory_space=pl.ANY)] * 3
+        + [pl.BlockSpec(memory_space=pltpu.SMEM)],
+        out_specs=pl.BlockSpec(memory_space=pl.ANY),
+        scratch_shapes=[
+            pltpu.VMEM((rows, width), jnp.bfloat16),
+            pltpu.VMEM((2, 6 * rows, width), jnp.bfloat16),
+            pltpu.VMEM((rows, width), jnp.bfloat16),
+            pltpu.SemaphoreType.DMA((3,)),
+            pltpu.SemaphoreType.DMA((chunks,)),
+            pltpu.SemaphoreType.DMA((7, chunks)),
+            pltpu.SemaphoreType.DMA((7, chunks)),
+        ],
+        compiler_params=pltpu.CompilerParams(
+            collective_id=0, has_side_effects=True, vmem_limit_bytes=48 * 2**20
+        ),
+        cost_estimate=pl.CostEstimate(
+            flops=24 * rows * rows * width,
+            bytes_accessed=10 * rows * width,
+            transcendentals=6 * rows * rows * heads,
+        ),
+    )(query_in, key_in, value_in, block_keep)
+
+
 def solution(mesh):
+    in_one_row = mesh.shape["ctx"] == COLS // TILE_S
     return jax.shard_map(
-        local,
+        one_row if in_one_row else local,
         mesh=mesh,
         in_specs=(
             P(("clips", "ctx", "head"), None),

time: 192 us -> 47.6 us (0.25)
  the two profiles are of different devices: /device:TPU:25 before, /device:TPU:11 now
where the time goes in v1:
time: 47.6 us; the launch traced here: 46.8 us
  Pallas kernels  41.9 us (88%)
  local copies, waits for them, and re-layouts  4.88 us (10%)
    pallas_call x1, Pallas kernels, one_row(): pl.pallas_call(functools.partial(row_kernel, lax.axis_size('ctx'), heads_...  41.9 us
    unnamed x8, local copies, waits for them, and re-layouts  4.88 us

profile of v1, /device:TPU:11, one launch (start us, length us, event | category | flops | bytes accessed | tf_op | source)
XLA Modules:
  0.0 46.8 jit_solution(3784485337004720029)
XLA Ops:
  0.0 0.8 %copy.5.keep = s32[1,1,8,3,3]{4,3,2,1,0:T(4,128)S(1)} copy(s32[1,1,8,3,3]{2,1,4,3,0:T(1,128)} %param.7) | data formatting | bytes 576 | tf_op args[3]
  0.8 0.0 copy-start
  0.8 1.1 %copy-done = bf16[128,2560]{1,0:T(8,128)(2,1)S(1)} copy-done((bf16[128,2560]{1,0:T(8,128)(2,1)S(1)}, bf16[128,2560]{1,0:T(8,128)(2,1)}, u32[]{:S(2)}) %copy-start) | copy-done | bytes 655384
  1.9 0.0 copy-start.1
  1.9 1.1 %copy-done.1 = bf16[128,2560]{1,0:T(8,128)(2,1)S(1)} copy-done((bf16[128,2560]{1,0:T(8,128)(2,1)S(1)}, bf16[128,2560]{1,0:T(8,128)(2,1)}, u32[]{:S(2)}) %copy-start.1) | copy-done | bytes 655384
  3.0 0.0 copy-start.2
  3.0 1.1 %copy-done.2 = bf16[128,2560]{1,0:T(8,128)(2,1)S(1)} copy-done((bf16[128,2560]{1,0:T(8,128)(2,1)S(1)}, bf16[128,2560]{1,0:T(8,128)(2,1)}, u32[]{:S(2)}) %copy-start.2) | copy-done | bytes 655384
  4.0 41.9 %shard_map.46 = bf16[128,2560]{1,0:T(8,128)(2,1)S(1)} custom-call(bf16[128,2560]{1,0:T(8,128)(2,1)S(1)} %copy-done, bf16[128,2560]{1,0:T(8,128)(2,1)S(1)} %copy-done.1, bf16[128,2560]{1,0:T(8,128)(2,1)S(1)} %copy-done.2, s32[1,1,8,3,3]{4,3,2,1,0:T(4,128)S(1)} %copy.5.keep), custom_call_target="tpu_custom_call" | custom-call | flops 1006632960 | bytes 3276800 | tf_op jit(solution)/shard_map/pallas_call | solution.py:432
  46.0 0.8 %copy.7 = bf16[128,2560]{1,0:T(8,128)(2,1)} copy(bf16[128,2560]{1,0:T(8,128)(2,1)S(1)} %shard_map.46) | data formatting | bytes 1310720
Async XLA Ops:
  0.8 1.1 %copy-start = (bf16[128,2560]{1,0:T(8,128)(2,1)S(1)}, bf16[128,2560]{1,0:T(8,128)(2,1)}, u32[]{:S(2)}) copy-start(bf16[128,2560]{1,0:T(8,128)(2,1)} %query_in.1) | copy-start | bytes 1966084
  1.9 1.1 %copy-start.1 = (bf16[128,2560]{1,0:T(8,128)(2,1)S(1)}, bf16[128,2560]{1,0:T(8,128)(2,1)}, u32[]{:S(2)}) copy-start(bf16[128,2560]{1,0:T(8,128)(2,1)} %key_in.1) | copy-start | bytes 1966084
  3.0 1.1 %copy-start.2 = (bf16[128,2560]{1,0:T(8,128)(2,1)S(1)}, bf16[128,2560]{1,0:T(8,128)(2,1)}, u32[]{:S(2)}) copy-start(bf16[128,2560]{1,0:T(8,128)(2,1)} %value_in.1) | copy-start | bytes 1966084

commit v2 on v1

--- a/solution.py
+++ b/solution.py
@@ -228,41 +228,38 @@
 
 
 HEADS_A_CHUNK = 2
+VMEM_LIMIT = 60 * 2**20
 LOG2_E = 1.4426950408889634
 MESH = pl.DeviceIdType.MESH
-OWN, CORE, BESIDE, BESIDE_CORE, FAR, FAR_CORE = range(6)
-
-
-def attend(query, keys, values, beside_ok, far_ok, tile_tok):
+OWN, CORE, BESIDE, FAR, BESIDE_CORE, FAR_CORE = range(6)
+
+
+def attend(query, keys, values, beside_ok, far_ok, rows):
     scale = HD ** (-0.5) * LOG2_E
     scores = lax.dot_general(
         query, keys, (((1,), (1,)), ((), ())), preferred_element_type=jnp.float32
     )
-    own, beside, far = (scores[:, i * tile_tok : (i + 1) * tile_tok] for i in range(3))
+    halves = [scores[:, slot * rows : (slot + 1) * rows] for slot in range(6)]
+    own = jnp.maximum(halves[OWN], halves[CORE])
+    beside = jnp.maximum(halves[BESIDE], halves[BESIDE_CORE])
+    far = jnp.maximum(halves[FAR], halves[FAR_CORE])
     row_max = jnp.maximum(
-        own.max(-1, keepdims=True),
-        jnp.maximum(
-            jnp.where(beside_ok, beside.max(-1, keepdims=True), NEG_BIG),
-            jnp.where(far_ok, far.max(-1, keepdims=True), NEG_BIG),
-        ),
-    )
-    weights = jnp.concatenate(
-        [
-            jnp.exp2((own - row_max) * scale),
-            jnp.exp2((beside - jnp.where(beside_ok, row_max, -NEG_BIG)) * scale),
-            jnp.exp2((far - jnp.where(far_ok, row_max, -NEG_BIG)) * scale),
-        ],
-        axis=1,
-    )
-    row_sum = weights.sum(-1, keepdims=True)
-    mixed = jnp.dot(weights.astype(jnp.bfloat16), values, preferred_element_type=jnp.float32)
+        own, jnp.maximum(jnp.where(beside_ok, beside, NEG_BIG), jnp.where(far_ok, far, NEG_BIG))
+    ).max(-1, keepdims=True)
+    beside_max = jnp.where(beside_ok, row_max, -NEG_BIG)
+    far_max = jnp.where(far_ok, row_max, -NEG_BIG)
+    tops = (row_max, row_max, beside_max, far_max, beside_max, far_max)
+    weights = [jnp.exp2((half - top) * scale) for half, top in zip(halves, tops)]
+    row_sum = sum(weights[1:], weights[0]).sum(-1, keepdims=True)
+    weights_b = jnp.concatenate([w.astype(jnp.bfloat16) for w in weights], axis=1)
+    mixed = jnp.dot(weights_b, values, preferred_element_type=jnp.float32)
     return (mixed / row_sum).astype(jnp.bfloat16)
 
 
 def row_kernel(
     tiles, heads_a_chunk,
     query_in, key_in, value_in, keep, out,
-    query, pairs, result, load_sem, store_sem, send_sem, recv_sem,
+    query, pairs, result, load_sem, store_sem, send_sem, core_sem, paired_sem, far_sem, relay_sem,
 ):
     rows = query_in.shape[0]
     chunks = query_in.shape[1] // (heads_a_chunk * HD)
@@ -275,55 +272,48 @@
     gets_far = jnp.logical_and(from_far >= 0, from_far < tiles)
     other_core = (clip, tile, 1 - core)
     paired = (clip, tile + 1 - 2 * side, core)
-    beyond = (clip, jnp.where(sends_far, to_far, tile), core)
-    behind = (clip, jnp.where(gets_far, from_far, tile), core)
-
-    def place(slot):
-        return pl.ds(slot * rows, rows)
+    beyond = (clip, jnp.where(sends_far, to_far, tile + 1 - 2 * side), core)
+    behind = (clip, jnp.where(gets_far, from_far, tile + 1 - 2 * side), core)
+
+    def place(slot, count=1):
+        return pl.ds(slot * rows, count * rows)
 
     def columns(chunk):
         return pl.ds(pl.multiple_of(chunk * width, width), width)
 
-    def own_copy(which, kind, slot, device, chunk):
-        source = (key_in, value_in)[which]
+    everything = slice(None)
+
+    def own_copy(which, slot, device, at, sender, receiver):
         return pltpu.make_async_remote_copy(
-            src_ref=source.at[:, columns(chunk)],
-            dst_ref=pairs.at[which, place(slot), columns(chunk)],
-            send_sem=send_sem.at[kind + which, chunk],
-            recv_sem=recv_sem.at[kind + which, chunk],
+            src_ref=(key_in, value_in)[which].at[:, at],
+            dst_ref=pairs.at[which, place(slot), at],
+            send_sem=send_sem.at[sender],
+            recv_sem=receiver,
             device_id=device,
             device_id_type=MESH,
         )
 
-    def relay(kind, source, slot, device, chunk):
+    def relay(source, slot, count, device, at, sender, receiver):
         return pltpu.make_async_remote_copy(
-            src_ref=pairs.at[:, place(source), columns(chunk)],
-            dst_ref=pairs.at[:, place(slot), columns(chunk)],
-            send_sem=send_sem.at[kind, chunk],
-            recv_sem=recv_sem.at[kind, chunk],
+            src_ref=pairs.at[:, place(source, count), at],
+            dst_ref=pairs.at[:, place(slot, count), at],
+            send_sem=send_sem.at[sender],
+            recv_sem=receiver,
             device_id=device,
             device_id_type=MESH,
         )
 
-    def to_core(which, chunk):
-        return own_copy(which, 0, CORE, other_core, chunk)
-
-    def to_paired(which, chunk):
-        return own_copy(which, 2, BESIDE, paired, chunk)
-
-    def paired_to_core(chunk):
-        return relay(4, BESIDE, BESIDE_CORE, other_core, chunk)
-
-    def paired_to_far(chunk):
-        return relay(5, BESIDE, FAR, beyond, chunk)
-
-    def far_to_core(chunk):
-        return relay(6, FAR, FAR_CORE, other_core, chunk)
-
-    def store(chunk):
-        return pltpu.make_async_copy(
-            result.at[:, columns(chunk)], out.at[:, columns(chunk)], store_sem.at[chunk]
-        )
+    def to_far_tile(chunk):
+        return relay(BESIDE, FAR, 1, beyond, columns(chunk), 2, far_sem.at[chunk])
+
+    def to_other_core(chunk):
+        return relay(BESIDE, BESIDE_CORE, 2, other_core, columns(chunk), 3, relay_sem.at[chunk])
+
+    def both_arrived(slot, at, receiver):
+        relay(slot, slot, 1, paired, at, 0, receiver).wait_recv()
+
+    def store(at):
+        return pltpu.make_async_copy(result.at[:, at], out.at[:, at], store_sem)
 
     loads = (
         pltpu.make_async_copy(query_in, query, load_sem.at[0]),
@@ -332,7 +322,6 @@
     )
 
     barrier = pltpu.get_barrier_semaphore()
-    pl.semaphore_signal(barrier, inc=1, device_id=other_core, device_id_type=MESH)
     pl.semaphore_signal(barrier, inc=1, device_id=paired, device_id_type=MESH)
 
     @pl.when(sends_far)
@@ -343,14 +332,14 @@
     def _():
         pl.semaphore_signal(barrier, inc=1, device_id=behind, device_id_type=MESH)
 
+    pl.semaphore_signal(barrier, inc=1, device_id=other_core, device_id_type=MESH)
+
     for load in loads:
         load.start()
 
     @pl.when(jnp.logical_not(gets_far))
     def _():
-        pairs[:, pl.ds(FAR * rows, 2 * rows), :] = jnp.zeros(
-            (2, 2 * rows, pairs.shape[2]), pairs.dtype
-        )
+        pairs[:, place(FAR), :] = jnp.zeros((2, rows, pairs.shape[2]), pairs.dtype)
 
     pl.semaphore_wait(
         barrier, 2 + sends_far.astype(jnp.int32) + gets_far.astype(jnp.int32)
@@ -359,69 +348,58 @@
     @pl.loop(0, chunks)
     def _(chunk):
         for which in range(2):
-            to_paired(which, chunk).start()
-        for which in range(2):
-            to_core(which, chunk).start()
+            own_copy(which, BESIDE, paired, columns(chunk), 0, paired_sem.at[chunk]).start()
+
+    for which in range(2):
+        own_copy(which, CORE, other_core, everything, 1, core_sem).start()
+
+    beside_ok = jnp.where(side == 0, keep[0, 1, 2, 0, tile], keep[0, 1, 0, 0, tile]) > 0
+    far_ok = jnp.logical_and(
+        jnp.where(side == 0, keep[0, 1, 0, 0, tile], keep[0, 1, 2, 0, tile]) > 0, gets_far
+    )
 
     for load in loads:
         load.wait()
-
-    beside_ok = jnp.where(side == 0, keep[0, 0, tile, 1, 2], keep[0, 0, tile, 1, 0]) > 0
-    far_ok = jnp.logical_and(
-        jnp.where(side == 0, keep[0, 0, tile, 1, 0], keep[0, 0, tile, 1, 2]) > 0, gets_far
-    )
+    both_arrived(CORE, everything, core_sem)
 
     @pl.loop(0, chunks + 2)
     def _(turn):
         @pl.when(turn < chunks)
         def _():
-            for which in range(2):
-                to_paired(which, turn).wait_recv()
-            paired_to_core(turn).start()
+            both_arrived(BESIDE, columns(turn), paired_sem.at[turn])
 
             @pl.when(sends_far)
             def _():
-                paired_to_far(turn).start()
-
-        @pl.when(jnp.logical_and(jnp.logical_and(turn >= 1, turn <= chunks), gets_far))
+                to_far_tile(turn).start()
+
+        @pl.when(jnp.logical_and(turn >= 1, turn <= chunks))
         def _():
-            paired_to_far(turn - 1).wait_recv()
-            far_to_core(turn - 1).start()
+            @pl.when(gets_far)
+            def _():
+                to_far_tile(turn - 1).wait_recv()
+
+            to_other_core(turn - 1).start()
 
         @pl.when(turn >= 2)
         def _():
             chunk = turn - 2
-            for which in range(2):
-                to_core(which, chunk).wait_recv()
-            paired_to_core(chunk).wait_recv()
-
-            @pl.when(gets_far)
-            def _():
-                far_to_core(chunk).wait_recv()
-
+            to_other_core(chunk).wait_recv()
             for head in range(heads_a_chunk):
                 at = pl.ds(pl.multiple_of(chunk * width + head * HD, HD), HD)
                 result[:, at] = attend(
-                    query[:, at], pairs[0, :, at], pairs[1, :, at], beside_ok, far_ok, 2 * rows
+                    query[:, at], pairs[0, :, at], pairs[1, :, at], beside_ok, far_ok, rows
                 )
-            store(chunk).start()
-
-    @pl.loop(0, chunks)
-    def _(chunk):
-        for which in range(2):
-            to_core(which, chunk).wait_send()
-            to_paired(which, chunk).wait_send()
-        paired_to_core(chunk).wait_send()
-
-        @pl.when(sends_far)
-        def _():
-            paired_to_far(chunk).wait_send()
-
-        @pl.when(gets_far)
-        def _():
-            far_to_core(chunk).wait_send()
-
-        store(chunk).wait()
+            store(columns(chunk)).start()
+
+    relay(BESIDE, BESIDE, 1, paired, everything, 0, core_sem).wait_send()
+    relay(BESIDE, BESIDE, 1, paired, everything, 1, core_sem).wait_send()
+    relay(BESIDE, BESIDE, 2, paired, everything, 3, core_sem).wait_send()
+
+    @pl.when(sends_far)
+    def _():
+        relay(BESIDE, BESIDE, 1, paired, everything, 2, core_sem).wait_send()
+
+    store(everything).wait()
 
 
 def one_row(query_in, key_in, value_in, block_keep):
@@ -431,7 +409,7 @@
     chunks = heads // heads_a_chunk
     return pl.pallas_call(
         functools.partial(row_kernel, lax.axis_size("ctx"), heads_a_chunk),
-        out_shape=jax.ShapeDtypeStruct((rows, width), jnp.bfloat16),
+        out_shape=pltpu.VMEM((rows, width), jnp.bfloat16),
         in_specs=[pl.BlockSpec(memory_space=pl.ANY)] * 3
         + [pl.BlockSpec(memory_space=pltpu.SMEM)],
         out_specs=pl.BlockSpec(memory_space=pl.ANY),
@@ -440,19 +418,22 @@
             pltpu.VMEM((2, 6 * rows, width), jnp.bfloat16),
             pltpu.VMEM((rows, width), jnp.bfloat16),
             pltpu.SemaphoreType.DMA((3,)),
+            pltpu.SemaphoreType.DMA,
+            pltpu.SemaphoreType.DMA((4,)),
+            pltpu.SemaphoreType.DMA,
             pltpu.SemaphoreType.DMA((chunks,)),
-            pltpu.SemaphoreType.DMA((7, chunks)),
-            pltpu.SemaphoreType.DMA((7, chunks)),
+            pltpu.SemaphoreType.DMA((chunks,)),
+            pltpu.SemaphoreType.DMA((chunks,)),
         ],
         compiler_params=pltpu.CompilerParams(
-            collective_id=0, has_side_effects=True, vmem_limit_bytes=48 * 2**20
+            collective_id=0, has_side_effects=True, vmem_limit_bytes=VMEM_LIMIT
         ),
         cost_estimate=pl.CostEstimate(
             flops=24 * rows * rows * width,
             bytes_accessed=10 * rows * width,
             transcendentals=6 * rows * rows * heads,
         ),
-    )(query_in, key_in, value_in, block_keep)
+    )(query_in, key_in, value_in, block_keep.transpose(0, 3, 4, 1, 2))
 
 
 def solution(mesh):

time: 47.6 us -> 42.4 us (0.89)
  local copies, waits for them, and re-layouts: 4.88 us -> 0.84 us
  Pallas kernels: 41.9 us -> 41.1 us
    unnamed x8 -> x1, local copies, waits for them, and re-layouts: 4.88 us -> 0.84 us
    pallas_call x1, Pallas kernels: 41.9 us -> 41.1 us  [one_row(): pl.pallas_call(functools.partial(row_kernel, lax.axis_size('ctx'), heads_...]
where the time goes in v2:
time: 42.4 us; the launch traced here: 41.9 us
  Pallas kernels  41.1 us (97%)
  local copies, waits for them, and re-layouts  0.84 us (2%)
    pallas_call x1, Pallas kernels, one_row(): pl.pallas_call(functools.partial(row_kernel, lax.axis_size('ctx'), heads_...  41.1 us

profile of v2, /device:TPU:11, one launch (start us, length us, event | category | flops | bytes accessed | tf_op | source)
XLA Modules:
  0.0 41.9 jit_solution(2338676360930809102)
XLA Ops:
  0.0 41.1 %shard_map.46 = bf16[128,2560]{1,0:T(8,128)(2,1)S(1)} custom-call(bf16[128,2560]{1,0:T(8,128)(2,1)} %query_in.1, bf16[128,2560]{1,0:T(8,128)(2,1)} %key_in.1, bf16[128,2560]{1,0:T(8,128)(2,1)} %value_in.1, s32[1,3,3,1,8]{4,3,2,1,0:T(1,128)} %bitcast.1), custom_call_target="tpu_custom_call" | custom-call | flops 1006632960 | bytes 3276800 | tf_op jit(solution)/shard_map/pallas_call | solution.py:410
  41.1 0.8 %copy.6 = bf16[128,2560]{1,0:T(8,128)(2,1)} copy(bf16[128,2560]{1,0:T(8,128)(2,1)S(1)} %shard_map.46) | data formatting | bytes 1310720

commit v3 on v2

--- a/solution.py
+++ b/solution.py
@@ -227,7 +227,9 @@
     return lax.all_to_all(whole_tile, "head", split_axis=0, concat_axis=1, tiled=True)
 
 
-HEADS_A_CHUNK = 2
+HEADS_A_CHUNK = 1
+FAR_LAG = 3
+ATTEND_LAG = 5
 VMEM_LIMIT = 60 * 2**20
 LOG2_E = 1.4426950408889634
 MESH = pl.DeviceIdType.MESH
@@ -258,8 +260,8 @@
 
 def row_kernel(
     tiles, heads_a_chunk,
-    query_in, key_in, value_in, keep, out,
-    query, pairs, result, load_sem, store_sem, send_sem, core_sem, paired_sem, far_sem, relay_sem,
+    query_in, key_in, value_in, keep_in, result,
+    query, pairs, keep, load_sem, send_sem, core_sem, paired_sem, far_sem, relay_sem,
 ):
     rows = query_in.shape[0]
     chunks = query_in.shape[1] // (heads_a_chunk * HD)
@@ -312,10 +314,8 @@
     def both_arrived(slot, at, receiver):
         relay(slot, slot, 1, paired, at, 0, receiver).wait_recv()
 
-    def store(at):
-        return pltpu.make_async_copy(result.at[:, at], out.at[:, at], store_sem)
-
     loads = (
+        pltpu.make_async_copy(keep_in, keep, load_sem.at[3]),
         pltpu.make_async_copy(query_in, query, load_sem.at[0]),
         pltpu.make_async_copy(key_in, pairs.at[0, place(OWN)], load_sem.at[1]),
         pltpu.make_async_copy(value_in, pairs.at[1, place(OWN)], load_sem.at[2]),
@@ -353,16 +353,15 @@
     for which in range(2):
         own_copy(which, CORE, other_core, everything, 1, core_sem).start()
 
+    for load in loads:
+        load.wait()
     beside_ok = jnp.where(side == 0, keep[0, 1, 2, 0, tile], keep[0, 1, 0, 0, tile]) > 0
     far_ok = jnp.logical_and(
         jnp.where(side == 0, keep[0, 1, 0, 0, tile], keep[0, 1, 2, 0, tile]) > 0, gets_far
     )
-
-    for load in loads:
-        load.wait()
     both_arrived(CORE, everything, core_sem)
 
-    @pl.loop(0, chunks + 2)
+    @pl.loop(0, chunks + ATTEND_LAG)
     def _(turn):
         @pl.when(turn < chunks)
         def _():
@@ -372,24 +371,23 @@
             def _():
                 to_far_tile(turn).start()
 
-        @pl.when(jnp.logical_and(turn >= 1, turn <= chunks))
+        @pl.when(jnp.logical_and(turn >= FAR_LAG, turn < chunks + FAR_LAG))
         def _():
             @pl.when(gets_far)
             def _():
-                to_far_tile(turn - 1).wait_recv()
-
-            to_other_core(turn - 1).start()
-
-        @pl.when(turn >= 2)
+                to_far_tile(turn - FAR_LAG).wait_recv()
+
+            to_other_core(turn - FAR_LAG).start()
+
+        @pl.when(turn >= ATTEND_LAG)
         def _():
-            chunk = turn - 2
+            chunk = turn - ATTEND_LAG
             to_other_core(chunk).wait_recv()
             for head in range(heads_a_chunk):
                 at = pl.ds(pl.multiple_of(chunk * width + head * HD, HD), HD)
                 result[:, at] = attend(
                     query[:, at], pairs[0, :, at], pairs[1, :, at], beside_ok, far_ok, rows
                 )
-            store(columns(chunk)).start()
 
     relay(BESIDE, BESIDE, 1, paired, everything, 0, core_sem).wait_send()
     relay(BESIDE, BESIDE, 1, paired, everything, 1, core_sem).wait_send()
@@ -398,8 +396,6 @@
     @pl.when(sends_far)
     def _():
         relay(BESIDE, BESIDE, 1, paired, everything, 2, core_sem).wait_send()
-
-    store(everything).wait()
 
 
 def one_row(query_in, key_in, value_in, block_keep):
@@ -410,15 +406,13 @@
     return pl.pallas_call(
         functools.partial(row_kernel, lax.axis_size("ctx"), heads_a_chunk),
         out_shape=pltpu.VMEM((rows, width), jnp.bfloat16),
-        in_specs=[pl.BlockSpec(memory_space=pl.ANY)] * 3
-        + [pl.BlockSpec(memory_space=pltpu.SMEM)],
-        out_specs=pl.BlockSpec(memory_space=pl.ANY),
+        in_specs=[pl.BlockSpec(memory_space=pl.ANY)] * 4,
+        out_specs=pl.BlockSpec(memory_space=pltpu.VMEM),
         scratch_shapes=[
             pltpu.VMEM((rows, width), jnp.bfloat16),
             pltpu.VMEM((2, 6 * rows, width), jnp.bfloat16),
-            pltpu.VMEM((rows, width), jnp.bfloat16),
-            pltpu.SemaphoreType.DMA((3,)),
-            pltpu.SemaphoreType.DMA,
+            pltpu.SMEM((1, 3, 3) + block_keep.shape[1:3], jnp.int32),
+            pltpu.SemaphoreType.DMA((4,)),
             pltpu.SemaphoreType.DMA((4,)),
             pltpu.SemaphoreType.DMA,
             pltpu.SemaphoreType.DMA((chunks,)),

time: 42.4 us -> 39.2 us (0.925)
  Pallas kernels: 41.1 us -> 38.2 us
    pallas_call x1, Pallas kernels: 41.1 us -> 38.2 us  [one_row(): pl.pallas_call(functools.partial(row_kernel, lax.axis_size('ctx'), heads_...]
where the time goes in v3:
time: 39.2 us; the launch traced here: 39 us
  Pallas kernels  38.2 us (97%)
  local copies, waits for them, and re-layouts  0.84 us (2%)
    pallas_call x1, Pallas kernels, one_row(): pl.pallas_call(functools.partial(row_kernel, lax.axis_size('ctx'), heads_...  38.2 us
    unnamed x1, local copies, waits for them, and re-layouts  0.84 us

profile of v3, /device:TPU:11, one launch (start us, length us, event | category | flops | bytes accessed | tf_op | source)
XLA Modules:
  0.0 39.0 jit_solution(4458358722583965367)
XLA Ops:
  0.0 38.2 %shard_map.46 = bf16[128,2560]{1,0:T(8,128)(2,1)S(1)} custom-call(bf16[128,2560]{1,0:T(8,128)(2,1)} %query_in.1, bf16[128,2560]{1,0:T(8,128)(2,1)} %key_in.1, bf16[128,2560]{1,0:T(8,128)(2,1)} %value_in.1, s32[1,3,3,1,8]{4,3,2,1,0:T(1,128)} %bitcast.1), custom_call_target="tpu_custom_call" | custom-call | flops 1006632960 | bytes 3276800 | tf_op jit(solution)/shard_map/pallas_call | solution.py:406
  38.2 0.8 %copy.6 = bf16[128,2560]{1,0:T(8,128)(2,1)} copy(bf16[128,2560]{1,0:T(8,128)(2,1)S(1)} %shard_map.46) | data formatting | bytes 1310720

commit v4 on v3

--- a/solution.py
+++ b/solution.py
@@ -295,18 +295,18 @@
             device_id_type=MESH,
         )
 
-    def relay(source, slot, count, device, at, sender, receiver):
+    def relay(source, slot, count, device, at, sender, receiver, which=everything):
         return pltpu.make_async_remote_copy(
-            src_ref=pairs.at[:, place(source, count), at],
-            dst_ref=pairs.at[:, place(slot, count), at],
+            src_ref=pairs.at[which, place(source, count), at],
+            dst_ref=pairs.at[which, place(slot, count), at],
             send_sem=send_sem.at[sender],
             recv_sem=receiver,
             device_id=device,
             device_id_type=MESH,
         )
 
-    def to_far_tile(chunk):
-        return relay(BESIDE, FAR, 1, beyond, columns(chunk), 2, far_sem.at[chunk])
+    def to_far_tile(chunk, which=everything):
+        return relay(BESIDE, FAR, 1, beyond, columns(chunk), 2, far_sem.at[chunk], which)
 
     def to_other_core(chunk):
         return relay(BESIDE, BESIDE_CORE, 2, other_core, columns(chunk), 3, relay_sem.at[chunk])
@@ -348,28 +348,28 @@
     @pl.loop(0, chunks)
     def _(chunk):
         for which in range(2):
-            own_copy(which, BESIDE, paired, columns(chunk), 0, paired_sem.at[chunk]).start()
+            own_copy(which, BESIDE, paired, columns(chunk), 0, paired_sem.at[which, chunk]).start()
 
     for which in range(2):
         own_copy(which, CORE, other_core, everything, 1, core_sem).start()
 
-    for load in loads:
-        load.wait()
+    loads[0].wait()
     beside_ok = jnp.where(side == 0, keep[0, 1, 2, 0, tile], keep[0, 1, 0, 0, tile]) > 0
     far_ok = jnp.logical_and(
         jnp.where(side == 0, keep[0, 1, 0, 0, tile], keep[0, 1, 2, 0, tile]) > 0, gets_far
     )
-    both_arrived(CORE, everything, core_sem)
-
     @pl.loop(0, chunks + ATTEND_LAG)
     def _(turn):
         @pl.when(turn < chunks)
         def _():
-            both_arrived(BESIDE, columns(turn), paired_sem.at[turn])
-
-            @pl.when(sends_far)
-            def _():
-                to_far_tile(turn).start()
+            for which in range(2):
+                own_copy(
+                    which, BESIDE, paired, columns(turn), 0, paired_sem.at[which, turn]
+                ).wait_recv()
+
+                @pl.when(sends_far)
+                def _():
+                    to_far_tile(turn, which).start()
 
         @pl.when(jnp.logical_and(turn >= FAR_LAG, turn < chunks + FAR_LAG))
         def _():
@@ -378,6 +378,12 @@
                 to_far_tile(turn - FAR_LAG).wait_recv()
 
             to_other_core(turn - FAR_LAG).start()
+
+        @pl.when(turn == ATTEND_LAG)
+        def _():
+            for load in loads[1:]:
+                load.wait()
+            both_arrived(CORE, everything, core_sem)
 
         @pl.when(turn >= ATTEND_LAG)
         def _():
@@ -415,7 +421,7 @@
             pltpu.SemaphoreType.DMA((4,)),
             pltpu.SemaphoreType.DMA((4,)),
             pltpu.SemaphoreType.DMA,
-            pltpu.SemaphoreType.DMA((chunks,)),
+            pltpu.SemaphoreType.DMA((2, chunks)),
             pltpu.SemaphoreType.DMA((chunks,)),
             pltpu.SemaphoreType.DMA((chunks,)),
         ],

time: 39.2 us -> 38.3 us (0.977)
  Pallas kernels: 38.2 us -> 37.3 us
    pallas_call x1, Pallas kernels: 38.2 us -> 37.3 us  [one_row(): pl.pallas_call(functools.partial(row_kernel, lax.axis_size('ctx'), heads_...]
where the time goes in v4:
time: 38.3 us; the launch traced here: 38.2 us
  Pallas kernels  37.3 us (97%)
  local copies, waits for them, and re-layouts  0.84 us (2%)
    pallas_call x1, Pallas kernels, one_row(): pl.pallas_call(functools.partial(row_kernel, lax.axis_size('ctx'), heads_...  37.3 us
    unnamed x1, local copies, waits for them, and re-layouts  0.84 us

profile of v4, /device:TPU:11, one launch (start us, length us, event | category | flops | bytes accessed | tf_op | source)
XLA Modules:
  0.0 38.2 jit_solution(14641937080591334111)
XLA Ops:
  0.0 37.3 %shard_map.46 = bf16[128,2560]{1,0:T(8,128)(2,1)S(1)} custom-call(bf16[128,2560]{1,0:T(8,128)(2,1)} %query_in.1, bf16[128,2560]{1,0:T(8,128)(2,1)} %key_in.1, bf16[128,2560]{1,0:T(8,128)(2,1)} %value_in.1, s32[1,3,3,1,8]{4,3,2,1,0:T(1,128)} %bitcast.1), custom_call_target="tpu_custom_call" | custom-call | flops 1006632960 | bytes 3276800 | tf_op jit(solution)/shard_map/pallas_call | solution.py:412
  37.3 0.8 %copy.6 = bf16[128,2560]{1,0:T(8,128)(2,1)} copy(bf16[128,2560]{1,0:T(8,128)(2,1)S(1)} %shard_map.46) | data formatting | bytes 1310720

commit v5 on v4

--- a/solution.py
+++ b/solution.py
@@ -308,8 +308,10 @@
     def to_far_tile(chunk, which=everything):
         return relay(BESIDE, FAR, 1, beyond, columns(chunk), 2, far_sem.at[chunk], which)
 
-    def to_other_core(chunk):
-        return relay(BESIDE, BESIDE_CORE, 2, other_core, columns(chunk), 3, relay_sem.at[chunk])
+    def to_other_core(chunk, slot, count=1):
+        return relay(
+            slot, slot + 2, count, other_core, columns(chunk), 3, relay_sem.at[chunk]
+        )
 
     def both_arrived(slot, at, receiver):
         relay(slot, slot, 1, paired, at, 0, receiver).wait_recv()
@@ -371,13 +373,15 @@
                 def _():
                     to_far_tile(turn, which).start()
 
+            to_other_core(turn, BESIDE).start()
+
         @pl.when(jnp.logical_and(turn >= FAR_LAG, turn < chunks + FAR_LAG))
         def _():
             @pl.when(gets_far)
             def _():
                 to_far_tile(turn - FAR_LAG).wait_recv()
 
-            to_other_core(turn - FAR_LAG).start()
+            to_other_core(turn - FAR_LAG, FAR).start()
 
         @pl.when(turn == ATTEND_LAG)
         def _():
@@ -388,7 +392,7 @@
         @pl.when(turn >= ATTEND_LAG)
         def _():
             chunk = turn - ATTEND_LAG
-            to_other_core(chunk).wait_recv()
+            to_other_core(chunk, BESIDE, 2).wait_recv()
             for head in range(heads_a_chunk):
                 at = pl.ds(pl.multiple_of(chunk * width + head * HD, HD), HD)
                 result[:, at] = attend(

time: 38.3 us -> 38.2 us (level)
  no operation moved by 1% of the time
where the time goes in v5:
time: 38.2 us; the launch traced here: 38.1 us
  Pallas kernels  37.2 us (97%)
  local copies, waits for them, and re-layouts  0.84 us (2%)
    pallas_call x1, Pallas kernels, one_row(): pl.pallas_call(functools.partial(row_kernel, lax.axis_size('ctx'), heads_...  37.2 us
    unnamed x1, local copies, waits for them, and re-layouts  0.84 us

profile of v5, /device:TPU:11, one launch (start us, length us, event | category | flops | bytes accessed | tf_op | source)
XLA Modules:
  0.0 38.1 jit_solution(12354993373868499505)
XLA Ops:
  0.0 37.2 %shard_map.46 = bf16[128,2560]{1,0:T(8,128)(2,1)S(1)} custom-call(bf16[128,2560]{1,0:T(8,128)(2,1)} %query_in.1, bf16[128,2560]{1,0:T(8,128)(2,1)} %key_in.1, bf16[128,2560]{1,0:T(8,128)(2,1)} %value_in.1, s32[1,3,3,1,8]{4,3,2,1,0:T(1,128)} %bitcast.1), custom_call_target="tpu_custom_call" | custom-call | flops 1006632960 | bytes 3276800 | tf_op jit(solution)/shard_map/pallas_call | solution.py:416
  37.2 0.8 %copy.6 = bf16[128,2560]{1,0:T(8,128)(2,1)} copy(bf16[128,2560]{1,0:T(8,128)(2,1)S(1)} %shard_map.46) | data formatting | bytes 1310720

commit v6 on v5

--- a/solution.py
+++ b/solution.py
@@ -347,13 +347,13 @@
         barrier, 2 + sends_far.astype(jnp.int32) + gets_far.astype(jnp.int32)
     )
 
+    for which in range(2):
+        own_copy(which, CORE, other_core, everything, 1, core_sem).start()
+
     @pl.loop(0, chunks)
     def _(chunk):
         for which in range(2):
             own_copy(which, BESIDE, paired, columns(chunk), 0, paired_sem.at[which, chunk]).start()
-
-    for which in range(2):
-        own_copy(which, CORE, other_core, everything, 1, core_sem).start()
 
     loads[0].wait()
     beside_ok = jnp.where(side == 0, keep[0, 1, 2, 0, tile], keep[0, 1, 0, 0, tile]) > 0

time: 38.2 us -> 38.2 us (level)
  no operation moved by 1% of the time
where the time goes in v6:
time: 38.2 us; the launch traced here: 38.1 us
  Pallas kernels  37.2 us (97%)
  local copies, waits for them, and re-layouts  0.84 us (2%)
    pallas_call x1, Pallas kernels, one_row(): pl.pallas_call(functools.partial(row_kernel, lax.axis_size('ctx'), heads_...  37.2 us
    unnamed x1, local copies, waits for them, and re-layouts  0.84 us

profile of v6, /device:TPU:11, one launch (start us, length us, event | category | flops | bytes accessed | tf_op | source)
XLA Modules:
  0.0 38.1 jit_solution(15809217209311876515)
XLA Ops:
  0.0 37.2 %shard_map.46 = bf16[128,2560]{1,0:T(8,128)(2,1)S(1)} custom-call(bf16[128,2560]{1,0:T(8,128)(2,1)} %query_in.1, bf16[128,2560]{1,0:T(8,128)(2,1)} %key_in.1, bf16[128,2560]{1,0:T(8,128)(2,1)} %value_in.1, s32[1,3,3,1,8]{4,3,2,1,0:T(1,128)} %bitcast.1), custom_call_target="tpu_custom_call" | custom-call | flops 1006632960 | bytes 3276800 | tf_op jit(solution)/shard_map/pallas_call | solution.py:416
  37.2 0.8 %copy.6 = bf16[128,2560]{1,0:T(8,128)(2,1)} copy(bf16[128,2560]{1,0:T(8,128)(2,1)S(1)} %shard_map.46) | data formatting | bytes 1310720

commit v7 on v6

--- a/solution.py
+++ b/solution.py
@@ -336,8 +336,7 @@
 
     pl.semaphore_signal(barrier, inc=1, device_id=other_core, device_id_type=MESH)
 
-    for load in loads:
-        load.start()
+    loads[0].start()
 
     @pl.when(jnp.logical_not(gets_far))
     def _():
@@ -354,6 +353,9 @@
     def _(chunk):
         for which in range(2):
             own_copy(which, BESIDE, paired, columns(chunk), 0, paired_sem.at[which, chunk]).start()
+
+    for load in loads[1:]:
+        load.start()
 
     loads[0].wait()
     beside_ok = jnp.where(side == 0, keep[0, 1, 2, 0, tile], keep[0, 1, 0, 0, tile]) > 0

time: 38.2 us -> 38.2 us (level)
  no operation moved by 1% of the time
where the time goes in v7:
time: 38.2 us; the launch traced here: 38.1 us
  Pallas kernels  37.2 us (97%)
  local copies, waits for them, and re-layouts  0.84 us (2%)
    pallas_call x1, Pallas kernels, one_row(): pl.pallas_call(functools.partial(row_kernel, lax.axis_size('ctx'), heads_...  37.2 us
    unnamed x1, local copies, waits for them, and re-layouts  0.84 us

profile of v7, /device:TPU:11, one launch (start us, length us, event | category | flops | bytes accessed | tf_op | source)
XLA Modules:
  0.0 38.1 jit_solution(9141090796055072575)
XLA Ops:
  0.0 37.2 %shard_map.46 = bf16[128,2560]{1,0:T(8,128)(2,1)S(1)} custom-call(bf16[128,2560]{1,0:T(8,128)(2,1)} %query_in.1, bf16[128,2560]{1,0:T(8,128)(2,1)} %key_in.1, bf16[128,2560]{1,0:T(8,128)(2,1)} %value_in.1, s32[1,3,3,1,8]{4,3,2,1,0:T(1,128)} %bitcast.1), custom_call_target="tpu_custom_call" | custom-call | flops 1006632960 | bytes 3276800 | tf_op jit(solution)/shard_map/pallas_call | solution.py:418
  37.2 0.8 %copy.6 = bf16[128,2560]{1,0:T(8,128)(2,1)} copy(bf16[128,2560]{1,0:T(8,128)(2,1)S(1)} %shard_map.46) | data formatting | bytes 1310720
